TPU v7x, 512 devices: a whole 4x4x16 slice. The times are simulated.
512 devices in a mesh: stack: 16 (over y, x_lo, core), space: 32 (over x_hi, z).
Axes of the slice: x: 4 (x_hi: 2, x_lo: 2; x = x_hi * 2 + x_lo), y: 4, z: 16, core: 2. Of those that a mesh axis runs over, the one named last changes fastest.
Arguments:
- phases: float32 [576, 16, 32768], P('stack', None, 'space'), may hold values from -15 to 15
- pairs: int32 [576, 2], replicated, may hold values from 0 to 143, as said below
- ref_pixel: int32 [1], replicated, may hold values from 0 to 524287
- coherent: int32 [16, 32768], P(None, 'space'), may hold values 0 or 1
Outputs:
- screens: float32 [144, 32768], P('stack', 'space')
- residual: float32 [144, 16, 32768], P('stack', None, 'space')
Inputs may be any that keep to these rules, and one draw needn't show every extreme that they name: `pairs`: each row holds an earlier and a later date, at most 8 dates apart; every two consecutive dates form a pair.
All inputs are finite; a program needn't handle non-finite values. No bound on the sum of `coherent` on one device may be relied on, other than what follows from the above.
Results may differ from a plain program's by a relative error of at most 0.00013.
Values sent between devices are 32-bit elements; how exact they have to be, the bound alone decides.
No kernel may reach another device: no remote copies, remote signals or barrier semaphores. Data moves between devices by JAX's collectives and lax.ppermute only.
A program may use at most 64 MiB of HBM per device.

v0:
```python
import jax
import jax.numpy as jnp
from jax import lax
from jax.sharding import PartitionSpec as P

DATES = 144
TAU = 8


def broadcast(value, axis, source):
    kept = jnp.where(lax.axis_index(axis) == source, value, 0).astype(value.dtype)
    return lax.psum(kept, axis)


def padded(block, sides, width):
    for axis, dim in sides:
        count = lax.axis_size(axis)
        forward = [(i, i + 1) for i in range(count - 1)]
        backward = [(target, source) for source, target in forward]
        low = lax.ppermute(
            lax.slice_in_dim(block, block.shape[dim] - width, None, axis=dim), axis, forward
        )
        high = lax.ppermute(lax.slice_in_dim(block, 0, width, axis=dim), axis, backward)
        block = jnp.concatenate([low, block, high], axis=dim)
    return block


def design(pairs):
    date_ids = jnp.arange(DATES, dtype=jnp.int32)
    later_date = (pairs[:, 1:2] == date_ids[None, :]).astype(jnp.float32)
    earlier = (pairs[:, 0:1] == date_ids[None, :]).astype(jnp.float32)
    return later_date - earlier


def inverse(design_mat):
    normal = jnp.dot(
        design_mat.T,
        design_mat,
        precision=lax.Precision.HIGHEST,
        preferred_element_type=jnp.float32,
    )
    normal = normal + jnp.eye(DATES, dtype=jnp.float32)
    factor = jnp.linalg.cholesky(normal)
    return jax.scipy.linalg.cho_solve((factor, True), design_mat.T)


def smoother():
    date_steps = jnp.arange(DATES, dtype=jnp.float32)
    date_gap = date_steps[:, None] - date_steps[None, :]
    kernel = jnp.exp(-date_gap * date_gap / (2.0 * TAU * TAU))
    return kernel / jnp.sum(kernel, axis=1, keepdims=True)


def body(phases, pairs, ref_pixel, coherent):
    highest = lax.Precision.HIGHEST
    design_mat = design(pairs)
    inverse_op = inverse(design_mat)
    smooth = smoother()
    stack_count = lax.axis_size("stack")
    cols_local = phases.shape[2]
    total_cols = cols_local * lax.axis_size("space")
    flat_index = ref_pixel[0]
    ref_row = flat_index // total_cols
    ref_col = flat_index % total_cols
    owner_index = ref_col // cols_local
    local_col = ref_col % cols_local
    ref_phase = lax.dynamic_slice(
        phases, (jnp.int32(0), ref_row, local_col), (phases.shape[0], 1, 1)
    )
    ref_phase = broadcast(ref_phase, "space", owner_index)
    referenced = phases - ref_phase
    in_block = lax.all_to_all(referenced, "stack", split_axis=2, concat_axis=0, tiled=True)
    piece_shape = in_block.shape
    flattened = in_block.reshape(piece_shape[0], piece_shape[1] * piece_shape[2])
    series = jnp.dot(inverse_op, flattened, precision=highest, preferred_element_type=jnp.float32)
    modelled = jnp.dot(design_mat, series, precision=highest, preferred_element_type=jnp.float32)
    misfit = jnp.mean(jnp.square(flattened - modelled), axis=0)
    high_pass = series - jnp.dot(
        smooth, series, precision=highest, preferred_element_type=jnp.float32
    )
    high_pass = high_pass.reshape(DATES, piece_shape[1], piece_shape[2])
    tiled_fit = jnp.broadcast_to(
        misfit.reshape(1, piece_shape[1], piece_shape[2]),
        (stack_count, piece_shape[1], piece_shape[2]),
    )
    high_pass, tiled_fit = (high_pass, tiled_fit)
    high_dates = lax.all_to_all(high_pass, "stack", split_axis=0, concat_axis=2, tiled=True)
    misfit_all = lax.all_to_all(tiled_fit, "stack", split_axis=0, concat_axis=2, tiled=True)
    mask_f = coherent.astype(jnp.float32)
    weight = mask_f / (1.0 + misfit_all[0])
    weighted = jnp.einsum("mrc,rc->mc", high_dates, weight, precision=highest)
    weight_sum = jnp.sum(weight, axis=0, keepdims=True)
    half_width = cols_local // 4
    wide_num, wide_den = (
        padded(weighted, (("space", 1),), half_width),
        padded(weight_sum, (("space", 1),), half_width),
    )
    padded_idx = jnp.arange(cols_local + 2 * half_width, dtype=jnp.int32)[:, None]
    out_idx = jnp.arange(cols_local, dtype=jnp.int32)[None, :]
    box_band = ((padded_idx >= out_idx) & (padded_idx <= out_idx + 2 * half_width)).astype(
        jnp.float32
    )
    box_num = jnp.dot(wide_num, box_band, precision=highest, preferred_element_type=jnp.float32)
    box_den = jnp.dot(wide_den, box_band, precision=highest, preferred_element_type=jnp.float32)
    screens = box_num / (1.0 + box_den)
    residual = mask_f[None, :, :] * (high_dates - screens[:, None, :])
    return (screens, residual)


def solution(mesh):
    return jax.shard_map(
        body,
        mesh=mesh,
        in_specs=(P("stack", None, "space"), P(), P(), P(None, "space")),
        out_specs=(P("stack", "space"), P("stack", None, "space")),
        check_vma=False,
    )
```

profile of v0, /device:TPU:6, one launch (start us, length us, event | category | flops | bytes accessed | tf_op | source)
XLA Modules:
  0.0 251.0 jit_solution(10939810136108053599)
XLA Ops:
  2.8 82.3 %psum.7 = f32[36]{0:T(128)S(1)} all-reduce(f32[36]{0:T(128)S(1)} %fusion.39), channel_id=1, replica_groups=mesh['stack'=16,'space'=32] {'space'}, use_global_device_ids=true, to_apply=%region_0.1 | all-reduce | flops 36 | bytes 288 | tf_op jit(solution)/shard_map/psum | solution.py:12
  85.1 1.9 broadcast_subtract_fusion
  87.0 6.6 %copy.37 = f32[36,16,1024]{0,1,2:T(8,128)} copy(f32[36,16,1024]{2,1,0:T(8,128)S(1)} %broadcast_subtract_fusion) | data formatting | bytes 4718592 | tf_op jit(solution)/shard_map/sub | solution.py:71
  93.6 12.2 %reshape.110 = f32[16,1,36864]{2,1,0:T(1,128)} reshape(f32[1024,16,36]{2,1,0:T(8,128)} %bitcast.67) | data formatting | bytes 4718592
  105.7 6.6 %all-to-all-start = ((f32[16,1,36864]{2,1,0:T(1,128)}), f32[16,1,36864]{2,1,0:T(1,128)S(1)}, u32[]{:S(2)}, u32[]{:S(2)}) async-start(f32[16,1,36864]{2,1,0:T(1,128)} %reshape.110), calls=%async_computation | async-start | bytes 4718592 | tf_op jit(solution)/shard_map/all_to_all | solution.py:72
  114.1 11.7 %cholesky.51 = f32[128,128]{1,0:T(8,128)S(1)} custom-call(f32[128,128]{1,0:T(8,128)S(1)} %cholesky.124), custom_call_target="Cholesky" | custom-call | tf_op jit(solution)/shard_map/jit(cholesky)/cholesky | solution.py:43
  125.9 9.8 %custom-call.18 = f32[1,128,128]{1,2,0:T(8,128)S(1)} custom-call(f32[1,128,128]{2,1,0:T(8,128)S(1)} %get-tuple-element.29), custom_call_target="InvertDiagBlocksLowerTriangular" | custom-call | tf_op jit(solution)/shard_map/jit(cholesky)/cholesky | solution.py:43
  140.2 19.7 %custom-call.19 = f32[2,128,128]{1,2,0:T(8,128)S(1)} custom-call(f32[2,128,128]{2,1,0:T(8,128)S(1)} %pad_maximum_fusion), custom_call_target="InvertDiagBlocksLowerTriangular" | custom-call | tf_op jit(solution)/shard_map/jit(_cho_solve)/triangular_solve | solution.py:44
  164.4 8.4 %reduce.20 = f32[16,36864]{1,0:T(8,128)} reduce(f32[16,1,36864]{2,1,0:T(1,128)S(1)} %all-to-all-done, f32[]{:T(128)} %broadcast.211), dimensions={1}, to_apply=%all_to_all.31.reduce_sub_computation | reduce | bytes 4718596 | tf_op jit(solution)/shard_map/all_to_all | solution.py:72
  172.9 14.1 %reshape.111 = f32[1024,16,36]{2,1,0:T(8,128)} reshape(f32[16,36864]{1,0:T(8,128)} %reduce.20) | data formatting | bytes 4718592
  187.0 8.8 %copy.38 = f32[36,16,16,64]{3,1,0,2:T(8,128)} copy(f32[36,16,16,64]{0,1,3,2:T(8,128)} %bitcast.68) | data formatting | bytes 4718592 | tf_op jit(solution)/shard_map/all_to_all | solution.py:72
  195.7 4.0 %reshape.70 = f32[576,1024]{1,0:T(8,128)S(1)} reshape(f32[16,36,16,64]{3,2,1,0:T(8,128)} %bitcast.69) | data formatting | bytes 4718592 | tf_op jit(solution)/shard_map/reshape | solution.py:74
  199.7 1.8 fusion.10
  201.5 2.2 multiply_reduce_fusion
  204.5 5.7 %all-to-all-start.1 = ((f32[16,1,1024]{2,1,0:T(1,128)}), f32[16,1,1024]{2,1,0:T(1,128)S(1)}, u32[]{:S(2)}, u32[]{:S(2)}) async-start(f32[16,1,1024]{2,1,0:T(1,128)} %reshape.114), calls=%async_computation.1 | async-start | bytes 131072 | tf_op jit(solution)/shard_map/all_to_all | solution.py:88
  212.8 2.3 all-to-all-done.1
  215.2 4.8 %all-to-all-start.2 = ((f32[16,1,9216]{2,1,0:T(1,128)}), f32[16,1,9216]{2,1,0:T(1,128)S(1)}, u32[]{:S(2)}, u32[]{:S(2)}) async-start(f32[16,1,9216]{2,1,0:T(1,128)} %reshape.112), calls=%async_computation.2 | async-start | bytes 1179648 | tf_op jit(solution)/shard_map/all_to_all | solution.py:87
  221.0 1.9 collective-permute-start.3
  222.9 3.9 %collective-permute-start.2 = (f32[1,256]{1,0:T(1,128)S(1)}, f32[1,256]{1,0:T(1,128)S(1)}, u32[]{:S(2)}, u32[]{:S(2)}) collective-permute-start(f32[1,256]{1,0:T(1,128)S(1)} %get-tuple-element.32), channel_id=1, source_target_pairs={{0,1},{1,2},{2,3},{3,4},{4,5},{5,6},{6,7},{7,8},{8,9},{9,10},{10,1... | collective-permute-start | bytes 3080 | tf_op jit(solution)/shard_map/ppermute | solution.py:20
  226.9 5.1 %collective-permute-done.2 = f32[1,256]{1,0:T(1,128)S(1)} collective-permute-done((f32[1,256]{1,0:T(1,128)S(1)}, f32[1,256]{1,0:T(1,128)S(1)}, u32[]{:S(2)}, u32[]{:S(2)}) %collective-permute-start.2) | collective-permute-done | bytes 1056 | tf_op jit(solution)/shard_map/ppermute | solution.py:20
  233.7 2.0 reduce.21
  236.9 1.9 collective-permute-start.1
  238.8 3.9 %collective-permute-start = (f32[9,256]{1,0:T(8,128)S(1)}, f32[9,256]{1,0:T(8,128)S(1)}, u32[]{:S(2)}, u32[]{:S(2)}) collective-permute-start(f32[9,256]{1,0:T(8,128)S(1)} %get-tuple-element.26), channel_id=1, source_target_pairs={{0,1},{1,2},{2,3},{3,4},{4,5},{5,6},{6,7},{7,8},{8,9},{9,10},{10,1... | collective-permute-start | bytes 27656 | tf_op jit(solution)/shard_map/ppermute | solution.py:20
  242.8 5.3 %collective-permute-done = f32[9,256]{1,0:T(8,128)S(1)} collective-permute-done((f32[9,256]{1,0:T(8,128)S(1)}, f32[9,256]{1,0:T(8,128)S(1)}, u32[]{:S(2)}, u32[]{:S(2)}) %collective-permute-start) | collective-permute-done | bytes 9248 | tf_op jit(solution)/shard_map/ppermute | solution.py:20
  (67 shorter events, 20.7 us)
Async XLA Ops:
  105.7 6.6 %copy-start.3 = (s32[576,2]{0,1:T(2,128)S(1)}, s32[576,2]{0,1:T(2,128)}, u32[]{:S(2)}) copy-start(s32[576,2]{0,1:T(2,128)} %param.5) | copy-start | bytes 13828
  105.7 58.1 %all-to-all-start = ((f32[16,1,36864]{2,1,0:T(1,128)}), f32[16,1,36864]{2,1,0:T(1,128)S(1)}, u32[]{:S(2)}, u32[]{:S(2)}) async-start(f32[16,1,36864]{2,1,0:T(1,128)} %reshape.110), calls=%async_computation | async-start | bytes 4718592 | tf_op jit(solution)/shard_map/all_to_all | solution.py:72
  159.9 1.7 copy-start.1
  204.5 10.6 %all-to-all-start.1 = ((f32[16,1,1024]{2,1,0:T(1,128)}), f32[16,1,1024]{2,1,0:T(1,128)S(1)}, u32[]{:S(2)}, u32[]{:S(2)}) async-start(f32[16,1,1024]{2,1,0:T(1,128)} %reshape.114), calls=%async_computation.1 | async-start | bytes 131072 | tf_op jit(solution)/shard_map/all_to_all | solution.py:88
  211.3 9.7 %copy-start = (s32[16,1024]{1,0:T(8,128)S(1)}, s32[16,1024]{1,0:T(8,128)}, u32[]{:S(2)}) copy-start(s32[16,1024]{1,0:T(8,128)} %param.7) | copy-start | bytes 196612
  215.2 18.5 %all-to-all-start.2 = ((f32[16,1,9216]{2,1,0:T(1,128)}), f32[16,1,9216]{2,1,0:T(1,128)S(1)}, u32[]{:S(2)}, u32[]{:S(2)}) async-start(f32[16,1,9216]{2,1,0:T(1,128)} %reshape.112), calls=%async_computation.2 | async-start | bytes 1179648 | tf_op jit(solution)/shard_map/all_to_all | solution.py:87
  221.0 5.9 %collective-permute-start.3 = (f32[1,256]{1,0:T(1,128)S(1)}, f32[1,256]{1,0:T(1,128)S(1)}, u32[]{:S(2)}, u32[]{:S(2)}) collective-permute-start(f32[1,256]{1,0:T(1,128)S(1)} %get-tuple-element.33), channel_id=1, source_target_pairs={{1,0},{2,1},{3,2},{4,3},{5,4},{6,5},{7,6},{8,7},{9,8},{10,9},{11,1... | collective-permute-start | bytes 3080 | tf_op jit(solution)/shard_map/ppermute | solution.py:23
  222.9 9.1 %collective-permute-start.2 = (f32[1,256]{1,0:T(1,128)S(1)}, f32[1,256]{1,0:T(1,128)S(1)}, u32[]{:S(2)}, u32[]{:S(2)}) collective-permute-start(f32[1,256]{1,0:T(1,128)S(1)} %get-tuple-element.32), channel_id=1, source_target_pairs={{0,1},{1,2},{2,3},{3,4},{4,5},{5,6},{6,7},{7,8},{8,9},{9,10},{10,1... | collective-permute-start | bytes 3080 | tf_op jit(solution)/shard_map/ppermute | solution.py:20
  236.9 5.9 %collective-permute-start.1 = (f32[9,256]{1,0:T(8,128)S(1)}, f32[9,256]{1,0:T(8,128)S(1)}, u32[]{:S(2)}, u32[]{:S(2)}) collective-permute-start(f32[9,256]{1,0:T(8,128)S(1)} %get-tuple-element.27), channel_id=1, source_target_pairs={{1,0},{2,1},{3,2},{4,3},{5,4},{6,5},{7,6},{8,7},{9,8},{10,9},{11,1... | collective-permute-start | bytes 27656 | tf_op jit(solution)/shard_map/ppermute | solution.py:23
  238.8 9.2 %collective-permute-start = (f32[9,256]{1,0:T(8,128)S(1)}, f32[9,256]{1,0:T(8,128)S(1)}, u32[]{:S(2)}, u32[]{:S(2)}) collective-permute-start(f32[9,256]{1,0:T(8,128)S(1)} %get-tuple-element.26), channel_id=1, source_target_pairs={{0,1},{1,2},{2,3},{3,4},{4,5},{5,6},{6,7},{7,8},{8,9},{9,10},{10,1... | collective-permute-start | bytes 27656 | tf_op jit(solution)/shard_map/ppermute | solution.py:20
  249.8 0.9 copy-start.2
where the time goes:
time: 255 us; the launch traced here: 251 us
  blocking collectives  82.3 us (32%)
  other arithmetic  60.1 us (24%)
  local copies, waits for them, and re-layouts  50.4 us (20%)
  starting transfers between devices  28.8 us (11%)
  matrix products  13.3 us (5%)
  waiting for transfers between devices  12.7 us (5%)
  between operations  3.31 us (1%)
    psum x1, blocking collectives, broadcast(): return lax.psum(kept, axis)  82.3 us
    unnamed x14, local copies, waits for them, and re-layouts  29 us
    another operation x7, other arithmetic, inverse(): factor = jnp.linalg.cholesky(normal)  24.3 us
    another operation x6, other arithmetic, inverse(): return jax.scipy.linalg.cho_solve((factor, True), design_mat.T)  19.8 us
    ppermute x2, waiting for transfers between devices, padded(): lax.ppermute(lax.slice_in_dim(block, block.shape[dim] - width, None, axis...  10.4 us
    all_to_all x2, local copies, waits for them, and re-layouts, body(): lax.all_to_all(referenced, 'stack', split_axis=2, concat_axis=0, tiled=True)  9.3 us
    all_to_all x1, other arithmetic, body(): lax.all_to_all(referenced, 'stack', split_axis=2, concat_axis=0, tiled=True)  8.41 us
    ppermute x2, starting transfers between devices, padded(): lax.ppermute(lax.slice_in_dim(block, block.shape[dim] - width, None, axis...  7.84 us
  transfers between devices with their start and end apart: 7, of which 3 were waited for; matrix products, arithmetic and copies ran while one was open for 22% of the time, Pallas kernels for 0%

commit v1 on v0

v1 whole, which is shorter than its diff:
```python
import functools

import jax
import jax.numpy as jnp
from jax import lax
from jax.experimental import pallas as pl
from jax.experimental.pallas import tpu as pltpu
from jax.sharding import Mesh, PartitionSpec as P

IFGS = 576
DATES = 144
ROWS = 16
TAU = 8
HALF = 256
STACK = 16
OWN_IFGS = IFGS // STACK
OWN_DATES = DATES // STACK
COLS = 1024
SPACE = 32
SUB = 8
LANE = 128
GROUP = 16
OUT_ROWS = STACK * GROUP
SUMS = OWN_DATES + 1
PIECE = SUMS + GROUP // SUB
PIXELS = SUB * LANE
WIDE = 256

STACK_AXES = ("y", "x_lo", "core")
SPACE_AXES = ("x_hi", "z_hi", "z_lo")

F32 = jnp.float32
BF16 = jnp.bfloat16
HIGHEST = lax.Precision.HIGHEST
FILLS = 4
VMEM_LIMIT = 16 * 1024 * 1024
BIG_LIMIT = 60 * 1024 * 1024


def tile_of(piece):
    return (piece // 8) * SUB, (piece % 8) * LANE


def split2(value):
    first = value.astype(BF16)
    return first, (value - first.astype(F32)).astype(BF16)


def iota(shape, axis):
    return lax.broadcasted_iota(jnp.int32, shape, axis)


def full(memory_space=pltpu.VMEM):
    return pl.BlockSpec(memory_space=memory_space)


def pack_kernel(pixel_ref, space_ref, x_ref, out_ref, cand_ref, held, in_sems, out_sems):
    step = OWN_IFGS // FILLS
    fills, sends = [], []
    for i in range(FILLS):
        ifgs = pl.ds(i * step, step)
        fills.append(
            pltpu.make_async_copy(x_ref.at[ifgs], held.at[ifgs], in_sems.at[i])
        )
        fills[-1].start()
    for i in range(FILLS):
        ifgs = pl.ds(i * step, step)
        fills[i].wait()
        for piece in range(STACK):
            r, c = tile_of(piece)
            send = pltpu.make_async_copy(
                held.at[ifgs, pl.ds(r, SUB), pl.ds(c, LANE)],
                out_ref.at[piece, ifgs],
                out_sems.at[i, piece],
            )
            send.start()
            sends.append(send)
    flat = pixel_ref[0]
    row = flat // (SPACE * COLS)
    col = lax.rem(flat, COLS)
    row_tile = pl.multiple_of((row // SUB) * SUB, SUB)
    col_tile = pl.multiple_of((col // LANE) * LANE, LANE)
    is_owner = space_ref[0] == lax.rem(flat, SPACE * COLS) // COLS
    picked = held[:, pl.ds(row_tile, SUB), pl.ds(col_tile, LANE)]
    shape = (OWN_IFGS, SUB, LANE)
    here = (iota(shape, 1) == lax.rem(row, SUB)) & (iota(shape, 2) == lax.rem(col, LANE))
    here = here & is_owner
    picked = jnp.sum(jnp.where(here, picked, 0.0), axis=1)
    picked = jnp.concatenate([picked, jnp.zeros((LANE - OWN_IFGS, LANE), F32)], axis=0)
    rows = lax.dot_general(
        jnp.ones((SUB, LANE), F32),
        picked,
        (((1,), (1,)), ((), ())),
        precision=HIGHEST,
        preferred_element_type=F32,
    )
    cand_ref[...] = rows[:1]
    for send in sends:
        send.wait()


def operator_kernel(pairs_ref, design_ref, design_t_ref, op_ref):
    dates = iota((DATES, IFGS), 0)
    later = (pairs_ref[1:2, :] == dates).astype(F32)
    earlier = (pairs_ref[0:1, :] == dates).astype(F32)
    design_t = later - earlier
    design_t_ref[...] = design_t.astype(BF16)
    design_ref[...] = jnp.concatenate([design_t.T] * 2, axis=1).astype(BF16)
    normal = lax.dot_general(
        design_t.astype(BF16),
        design_t.astype(BF16),
        (((1,), (1,)), ((), ())),
        preferred_element_type=F32,
    )
    eye = (iota((DATES, DATES), 0) == iota((DATES, DATES), 1)).astype(F32)
    normal = normal + eye
    diag = jnp.sum(normal * eye, axis=0, keepdims=True)
    error = eye - normal / diag
    inverse = eye / diag
    bound = 14.0 * jnp.max(diag)
    mul = functools.partial(jnp.dot, precision=HIGHEST, preferred_element_type=F32)

    def step(carry):
        power, inv, err = carry
        return power * 2.0, inv + mul(inv, err), mul(err, err)

    _, inverse, _ = lax.while_loop(
        lambda carry: carry[0] < bound, step, (jnp.float32(1.0), inverse, error)
    )
    inverse = inverse + mul(inverse, eye - mul(normal, inverse))
    steps = iota((DATES, DATES), 0) - iota((DATES, DATES), 1)
    gauss = jnp.exp(-(steps * steps).astype(F32) / (2.0 * TAU * TAU))
    smooth = gauss / jnp.sum(gauss, axis=1, keepdims=True)
    high = mul(eye - smooth, inverse)
    out_row = iota((OUT_ROWS, DATES), 0)
    place = out_row & (GROUP - 1)
    date = jnp.where(place < OWN_DATES, (out_row >> 4) * OWN_DATES + place, -1)
    spread = (iota((OUT_ROWS, DATES), 1) == date).astype(F32)
    first, second = split2(jnp.concatenate([inverse, mul(spread, high)], axis=0))
    op_ref[...] = jnp.concatenate([first, second, first], axis=1)


def invert_kernel(
    place_ref, x_ref, refs_ref, design_ref, design_t_ref, op_ref, mask_ref, high_ref, sums_ref
):
    place = place_ref[0]
    row_tile = pl.multiple_of((place // 8) * SUB, SUB)
    col_tile = pl.multiple_of(lax.rem(place, 8) * LANE, LANE)
    coherent = mask_ref[pl.ds(row_tile, SUB), pl.ds(col_tile, LANE)].astype(F32)
    is_weight = (iota((OUT_ROWS, LANE), 0) & (GROUP - 1)) == OWN_DATES
    ifg = iota((IFGS, STACK), 0)
    spread = (iota((IFGS, STACK), 1) == (ifg * 1821) >> 16).astype(F32)
    refs = refs_ref[:STACK] + refs_ref[STACK:]
    refs = jnp.dot(spread, refs, precision=HIGHEST, preferred_element_type=F32)
    ifg = iota((IFGS, LANE), 0)
    own = iota((IFGS, LANE), 1) == ifg - ((ifg * 1821) >> 16) * OWN_IFGS
    ref_phase = jnp.sum(jnp.where(own, refs, 0.0), axis=1, keepdims=True)
    rows_at_once = WIDE // LANE
    dot = functools.partial(jnp.dot, preferred_element_type=F32)
    sums = jnp.zeros((OUT_ROWS, LANE), F32)
    for first in range(0, SUB, rows_at_once):
        rows = range(first, first + rows_at_once)
        x = jnp.concatenate([x_ref[pl.ds(r, IFGS, stride=SUB), :] for r in rows], axis=1)
        x = x - ref_phase
        moment, moment_rest = split2(sum(dot(design_t_ref[...], term) for term in split2(x)))
        both = dot(op_ref[...], jnp.concatenate([moment, moment, moment_rest], axis=0))
        model = dot(design_ref[...], jnp.concatenate(split2(both[:DATES]), axis=0))
        gap = x - model
        misfit = jnp.sum(gap * gap, axis=0, keepdims=True) * (1.0 / IFGS)
        for i, r in enumerate(rows):
            part = slice(i * LANE, (i + 1) * LANE)
            weight = coherent[r : r + 1] / (1.0 + misfit[:, part])
            high = jnp.where(is_weight, 1.0, both[DATES:, part])
            weighted = high * weight
            sums = sums + weighted
            high = jnp.where(is_weight, weighted, high)
            high_ref[:, r * LANE : (r + 1) * LANE] = high
    sums_ref[...] = sums


def pieces_kernel(high_ref, sums_ref, out_ref):
    for r in range(SUB):
        for t in range(STACK):
            out_ref[pl.ds(t * PIECE * SUB + r, SUMS, stride=SUB), :] = high_ref[
                t * GROUP : t * GROUP + SUMS, r * LANE : (r + 1) * LANE
            ]
    for t in range(STACK):
        last = t * PIECE * SUB + SUMS * SUB
        out_ref[last : last + GROUP] = sums_ref[t * GROUP : (t + 1) * GROUP]


def screen_kernel(x_ref, mask_ref, screens_ref, residual_ref):
    halves = range(ROWS // SUB)
    tiles = COLS // LANE

    def own(c):
        total = 0.0
        for half in halves:
            piece = x_ref[half * tiles + c]
            weight = piece[OWN_DATES:SUMS]
            part = jnp.concatenate([piece[:OWN_DATES] * weight, weight], axis=0)
            total = total + part
        total = jnp.sum(total, axis=1)
        return jnp.concatenate([total, jnp.zeros((GROUP - SUMS, LANE), F32)], axis=0)

    def neighbour(c):
        total = sum(x_ref[half * tiles + c, SUMS:] for half in halves)
        return total.reshape(GROUP, LANE)

    def block(part, first):
        return jnp.concatenate([part(first), part(first + 1)], axis=1)

    blocks = [block(neighbour, tiles - 2)]
    blocks += [block(own, c) for c in range(0, tiles, 2)]
    blocks += [block(neighbour, 0)]
    shape = (HALF, HALF)
    from_here = (iota(shape, 0) >= iota(shape, 1)).astype(BF16)
    up_to_here = (iota(shape, 0) <= iota(shape, 1)).astype(BF16)
    band = jnp.concatenate([from_here, jnp.ones(shape, BF16), up_to_here], axis=0)
    count = COLS // HALF
    wide = jnp.concatenate(
        [jnp.concatenate(blocks[i : i + 3], axis=1) for i in range(count)], axis=0
    )
    box = sum(jnp.dot(t, band, preferred_element_type=F32) for t in split2(wide))
    for i in range(count):
        sums = box[i * GROUP : (i + 1) * GROUP]
        screen = sums[:OWN_DATES] / (1.0 + sums[OWN_DATES:SUMS])
        screens_ref[:, i * HALF : (i + 1) * HALF] = screen
        for c in range(i * HALF, (i + 1) * HALF, LANE):
            part = screen[:, c - i * HALF : c - i * HALF + LANE]
            for half in halves:
                rows = slice(half * SUB, (half + 1) * SUB)
                mask = mask_ref[rows, c : c + LANE].astype(F32)
                residual_ref[:, rows, c : c + LANE] = mask[None] * (
                    x_ref[half * tiles + c // LANE][:OWN_DATES] - part[:, None, :]
                )


def call(kernel, out_shape, in_specs, out_specs, scratch=(), flops=0, nbytes=0, vmem=VMEM_LIMIT):
    return pl.pallas_call(
        kernel,
        out_shape=out_shape,
        in_specs=in_specs,
        out_specs=out_specs,
        scratch_shapes=scratch,
        compiler_params=pltpu.CompilerParams(vmem_limit_bytes=vmem),
        cost_estimate=pl.CostEstimate(flops=flops, bytes_accessed=nbytes, transcendentals=0),
    )


def struct(*shape, dtype=F32):
    return jax.ShapeDtypeStruct(shape, dtype)


def body(phases, pairs, ref_pixel, coherent):
    send, cand = call(
        pack_kernel,
        (struct(STACK, OWN_IFGS, SUB, LANE), struct(1, LANE)),
        [full(pltpu.SMEM), full(pltpu.SMEM), full(pltpu.HBM)],
        (full(pltpu.HBM), full()),
        [
            pltpu.VMEM((OWN_IFGS, ROWS, COLS), F32),
            pltpu.SemaphoreType.DMA((FILLS,)),
            pltpu.SemaphoreType.DMA((FILLS, STACK)),
        ],
        nbytes=2 * 4 * OWN_IFGS * ROWS * COLS,
        vmem=BIG_LIMIT,
    )(ref_pixel, lax.axis_index(SPACE_AXES).reshape(1), phases)
    block = lax.all_to_all(send, STACK_AXES, split_axis=0, concat_axis=0, tiled=True)

    design, design_t, operator = call(
        operator_kernel,
        (
            struct(IFGS, 2 * DATES, dtype=BF16),
            struct(DATES, IFGS, dtype=BF16),
            struct(DATES + OUT_ROWS, 3 * DATES, dtype=BF16),
        ),
        [full()],
        (full(), full(), full()),
        flops=30 * 6 * 2 * 256**3,
        nbytes=10**6,
    )(pairs.T)

    refs = cand
    for axis in ("z_lo", "z_hi"):
        refs = jnp.sum(lax.all_gather(refs, axis, axis=0, tiled=True), axis=0, keepdims=True)
    refs, block, operator = lax.optimization_barrier((refs, block, operator))
    refs = lax.all_to_all(
        jnp.broadcast_to(refs, (2 * STACK, LANE)),
        ("x_hi",) + STACK_AXES,
        split_axis=0,
        concat_axis=0,
        tiled=True,
    )

    high, sums = call(
        invert_kernel,
        (struct(OUT_ROWS, PIXELS), struct(OUT_ROWS, LANE)),
        [full(pltpu.SMEM)] + [full()] * 6,
        (full(), full()),
        flops=6 * 2 * PIXELS * DATES * 1200,
        nbytes=4 * (IFGS + OUT_ROWS) * PIXELS,
    )(
        lax.axis_index(STACK_AXES).reshape(1),
        block.reshape(IFGS * SUB, LANE),
        refs,
        design,
        design_t,
        operator,
        coherent,
    )

    count = SPACE
    tiles = COLS // LANE
    edge = HALF // LANE
    moves = []
    for s in range(STACK):
        step = -1 if s % tiles < edge else 1 if s % tiles >= tiles - edge else 0
        moves += [
            (s * count + i, s * count + i + step)
            for i in range(count)
            if step and 0 <= i + step < count
        ]
    beside = lax.ppermute(sums, STACK_AXES + SPACE_AXES, moves)

    pieces = call(
        pieces_kernel,
        struct(STACK * PIECE * SUB, LANE),
        [full()] * 2,
        full(),
        nbytes=4 * 2 * STACK * PIECE * PIXELS,
    )(high, beside)
    dated = lax.all_to_all(
        pieces.reshape(STACK, PIECE, SUB, LANE), STACK_AXES, split_axis=0, concat_axis=0, tiled=True
    )

    return call(
        screen_kernel,
        (struct(OWN_DATES, COLS), struct(OWN_DATES, ROWS, COLS)),
        [full()] * 2,
        (full(), full()),
        flops=2 * 64 * 768 * 256 * 3,
        nbytes=2 * 4 * PIECE * ROWS * COLS,
    )(dated, coherent)


def solution(mesh):
    fine = Mesh(mesh.devices.reshape(4, 2, 2, 2, 4, 4), STACK_AXES + SPACE_AXES)
    return jax.shard_map(
        body,
        mesh=fine,
        in_specs=(P(STACK_AXES, None, SPACE_AXES), P(), P(), P(None, SPACE_AXES)),
        out_specs=(P(STACK_AXES, SPACE_AXES), P(STACK_AXES, None, SPACE_AXES)),
        check_vma=False,
    )
```

time: 255 us -> 92 us (0.36); the launches traced: 251 us -> 91.2 us
  other arithmetic: 60.1 us -> 0.04 us
  local copies, waits for them, and re-layouts: 50.4 us -> 0.63 us
  blocking collectives: 82.3 us -> 56.1 us
  starting transfers between devices: 28.8 us -> 13.7 us
  Pallas kernels: 0 us -> 13.9 us
  matrix products: 13.3 us -> 0 us
  waiting for transfers between devices: 12.7 us -> 5.48 us
    psum x1 -> x0, blocking collectives: 82.3 us -> none  [broadcast(): return lax.psum(kept, axis)]
    another operation x13 -> x0, other arithmetic: 44.1 us -> none  [the longest x7 24.3 us: inverse(): factor = jnp.linalg.cholesky(normal)]
    all_gather x0 -> x2, blocking collectives: none -> 29.9 us  [body(): lax.all_gather(refs, axis, axis=0, tiled=True)]
    unnamed x14 -> x6, local copies, waits for them, and re-layouts: 29 us -> 0.02 us
    all_to_all x0 -> x1, blocking collectives: none -> 26.2 us  [body(): lax.all_to_all(pieces.reshape(STACK, PIECE, SUB, LANE), STACK_AXES, split...]
    pallas_call x0 -> x5, Pallas kernels: none -> 13.9 us  [the longest x1 5.31 us: body(): call(operator_kernel, (struct(IFGS, 2 * DATES, dtype=BF16), struct(DATES,...]
    all_to_all x3 -> x0, other arithmetic: 11.2 us -> none  [the longest x1 8.41 us: body(): lax.all_to_all(referenced, 'stack', split_axis=2, concat_axis=0, tiled=True)]
    ppermute x4 -> x1, starting transfers between devices: 11.7 us -> 0.67 us  [body(): beside = lax.ppermute(sums, STACK_AXES + SPACE_AXES, moves)]
  transfers between devices with their start and end apart: 7 -> 3, of which waited for: 3 -> 1; matrix products, arithmetic and copies ran while one was open for 22% -> 0% of each run, Pallas kernels for 0% -> 6%
where the time goes in v1:
time: 92 us; the launch traced here: 91.2 us
  blocking collectives  56.1 us (61%)
  Pallas kernels  13.9 us (15%)
  starting transfers between devices  13.7 us (15%)
  waiting for transfers between devices  5.48 us (6%)
  between operations  1.38 us (2%)
    all_gather x2, blocking collectives, body(): lax.all_gather(refs, axis, axis=0, tiled=True)  29.9 us
    all_to_all x1, blocking collectives, body(): lax.all_to_all(pieces.reshape(STACK, PIECE, SUB, LANE), STACK_AXES, split...  26.2 us
    all_to_all x1, starting transfers between devices, body(): lax.all_to_all(jnp.broadcast_to(refs, (2 * STACK, LANE)), ('x_hi',) + STA...  7.09 us
    all_to_all x1, starting transfers between devices, body(): lax.all_to_all(send, STACK_AXES, split_axis=0, concat_axis=0, tiled=True)  5.96 us
    all_to_all x1, waiting for transfers between devices, body(): lax.all_to_all(jnp.broadcast_to(refs, (2 * STACK, LANE)), ('x_hi',) + STA...  5.47 us
    pallas_call x1, Pallas kernels, body(): call(operator_kernel, (struct(IFGS, 2 * DATES, dtype=BF16), struct(DATES,...  5.31 us
    pallas_call x1, Pallas kernels, body(): call(pack_kernel, (struct(STACK, OWN_IFGS, SUB, LANE), struct(1, LANE)),...  3.6 us
    pallas_call x1, Pallas kernels, body(): call(invert_kernel, (struct(OUT_ROWS, PIXELS), struct(OUT_ROWS, LANE)), [...  3.55 us
  transfers between devices with their start and end apart: 3, of which 1 were waited for; matrix products, arithmetic and copies ran while one was open for 0% of the time, Pallas kernels for 6%

profile of v1, /device:TPU:6, one launch (start us, length us, event | category | flops | bytes accessed | tf_op | source)
XLA Modules:
  0.0 91.2 jit_solution(2713903505301361601)
XLA Ops:
  1.3 3.6 %shard_map.59 = (f32[16,36,8,128]{3,2,1,0:T(8,128)}, f32[1,128]{1,0:T(1,128)}) custom-call(s32[1]{0:T(128)S(6)} %copy.6.pixel_ref, s32[1]{0:T(128)} %bitcast.1.space_ref, f32[36,16,1024]{2,1,0:T(8,128)} %x_ref.1), custom_call_target="tpu_custom_call" | custom-call | bytes 4718592 | tf_op jit(solution)/shard_map/pallas_call | solution.py:256
  4.9 0.0 copy-start.2
  4.9 0.0 copy-start.1
  4.9 6.0 %all-to-all-start = ((f32[16,36,8,128]{3,2,1,0:T(8,128)}), f32[16,36,8,128]{3,2,1,0:T(8,128)S(1)}, u32[]{:S(2)}, u32[]{:S(2)}) async-start(f32[16,36,8,128]{3,2,1,0:T(8,128)} %get-tuple-element.13), calls=%async_computation | async-start | bytes 4718592 | tf_op jit(solution)/shard_map/all_to_all | solution.py:269
  10.9 0.0 copy-done.2
  10.9 12.1 %all-gather.1 = f32[4,1,128]{2,1,0:T(1,128)S(1)} all-gather(f32[1,1,128]{2,1,0:T(1,128)S(1)} %bitcast.15), channel_id=1, replica_groups=mesh['y'=4,'x_lo'=2,'core'=2,'x_hi'=2,'z_hi'=4,'z_lo'=4] {'z_lo'}, dimensions={0}, use_global_device_ids=true | all-gather | bytes 2560 | tf_op jit(solution)/shard_map/all_gather | solution.py:286
  23.0 17.7 %all-gather.2 = f32[4,1,128]{2,1,0:T(1,128)S(1)} all-gather(f32[1,1,128]{2,1,0:T(1,128)S(1)} %bitcast.14), channel_id=2, replica_groups=mesh['y'=4,'x_lo'=2,'core'=2,'x_hi'=2,'z_hi'=4,'z_lo'=4] {'z_hi'}, dimensions={0}, use_global_device_ids=true | all-gather | bytes 2560 | tf_op jit(solution)/shard_map/all_gather | solution.py:286
  40.8 0.0 copy-done.1
  40.8 0.0 copy-start
  40.8 5.3 %shard_map.60 = (bf16[576,288]{1,0:T(8,128)(2,1)S(1)}, bf16[144,576]{1,0:T(8,128)(2,1)S(1)}, bf16[400,432]{1,0:T(8,128)(2,1)S(1)}) custom-call(s32[2,576]{1,0:T(2,128)S(1)} %bitcast.13), custom_call_target="tpu_custom_call" | custom-call | flops 6039797760 | bytes 1000000 | tf_op jit(solution)/shard_map/pallas_call | solution.py:271
  46.1 0.0 all-to-all-done
  46.1 0.6 broadcast_in_dim.13
  46.7 7.1 %all-to-all-start.1 = ((f32[32,1,128]{2,1,0:T(1,128)}), f32[32,1,128]{2,1,0:T(1,128)S(1)}, u32[]{:S(2)}, u32[]{:S(2)}) async-start(f32[32,1,128]{2,1,0:T(1,128)} %broadcast_in_dim.13), calls=%async_computation.1 | async-start | bytes 32768 | tf_op jit(solution)/shard_map/all_to_all | solution.py:288
  53.8 5.5 %all-to-all-done.1 = f32[32,1,128]{2,1,0:T(1,128)S(1)} async-done(((f32[32,1,128]{2,1,0:T(1,128)}), f32[32,1,128]{2,1,0:T(1,128)S(1)}, u32[]{:S(2)}, u32[]{:S(2)}) %all-to-all-start.1) | async-done | bytes 16416 | tf_op jit(solution)/shard_map/all_to_all | solution.py:288
  59.3 0.0 copy-done
  59.3 3.6 %shard_map.61 = (f32[256,1024]{1,0:T(8,128)S(1)}, f32[256,128]{1,0:T(8,128)S(1)}) custom-call(s32[1]{0:T(128)} %bitcast.place_ref, f32[4608,128]{1,0:T(8,128)S(1)} %bitcast.11, f32[32,128]{1,0:T(8,128)S(1)} %bitcast.12, bf16[576,288]{1,0:T(8,128)(2,1)S(1)} %get-tuple-element.17.design_ref, bf16[144,576]{1,0:T(8,128)(2,1)S(1)} %get-tuple-element.18.design_t_ref, ...), custom_call_target="tpu_custom_call" | custom-call | flops 2123366400 | bytes 3407872 | tf_op jit(solution)/shard_map/pallas_call | solution.py:296
  62.9 0.7 collective-permute-start
  63.6 0.0 collective-permute-done.sums_ref
  63.6 0.2 shard_map.62
  63.8 26.2 %all_to_all.18.x_ref = f32[16,12,8,128]{3,2,1,0:T(8,128)S(1)} all-to-all(f32[16,12,8,128]{3,2,1,0:T(8,128)S(1)} %bitcast.10), channel_id=1, replica_groups=mesh['y'=4,'x_lo'=2,'core'=2,'x_hi'=2,'z_hi'=4,'z_lo'=4] {'y','x_lo','co..., dimensions={0} | all-to-all | bytes 1572864 | tf_op jit(solution)/shard_map/all_to_all | solution.py:333
  90.0 1.2 %shard_map.63 = (f32[9,1024]{1,0:T(8,128)}, f32[9,16,1024]{2,1,0:T(8,128)}) custom-call(f32[16,12,8,128]{3,2,1,0:T(8,128)S(1)} %all_to_all.18.x_ref, s32[16,1024]{1,0:T(8,128)S(1)} %copy-done), custom_call_target="tpu_custom_call" | custom-call | flops 75497472 | bytes 1572864 | tf_op jit(solution)/shard_map/pallas_call | solution.py:337
  (2 shorter events, 0.0 us)
Async XLA Ops:
  4.9 6.0 %copy-start.2 = (f32[1,128]{1,0:T(1,128)S(1)}, f32[1,128]{1,0:T(1,128)}, u32[]{:S(2)}) copy-start(f32[1,128]{1,0:T(1,128)} %get-tuple-element.12) | copy-start | bytes 1540
  4.9 35.9 %copy-start.1 = (s32[576,2]{0,1:T(2,128)S(1)}, s32[576,2]{0,1:T(2,128)}, u32[]{:S(2)}) copy-start(s32[576,2]{0,1:T(2,128)} %param.5) | copy-start | bytes 13828
  4.9 41.2 %all-to-all-start = ((f32[16,36,8,128]{3,2,1,0:T(8,128)}), f32[16,36,8,128]{3,2,1,0:T(8,128)S(1)}, u32[]{:S(2)}, u32[]{:S(2)}) async-start(f32[16,36,8,128]{3,2,1,0:T(8,128)} %get-tuple-element.13), calls=%async_computation | async-start | bytes 4718592 | tf_op jit(solution)/shard_map/all_to_all | solution.py:269
  40.8 18.5 %copy-start = (s32[16,1024]{1,0:T(8,128)S(1)}, s32[16,1024]{1,0:T(8,128)}, u32[]{:S(2)}) copy-start(s32[16,1024]{1,0:T(8,128)} %mask_ref.3) | copy-start | bytes 196612
  46.7 12.6 %all-to-all-start.1 = ((f32[32,1,128]{2,1,0:T(1,128)}), f32[32,1,128]{2,1,0:T(1,128)S(1)}, u32[]{:S(2)}, u32[]{:S(2)}) async-start(f32[32,1,128]{2,1,0:T(1,128)} %broadcast_in_dim.13), calls=%async_computation.1 | async-start | bytes 32768 | tf_op jit(solution)/shard_map/all_to_all | solution.py:288
  62.9 0.7 collective-permute-start

commit v2 on v1

--- a/solution.py
+++ b/solution.py
@@ -34,7 +34,7 @@
 HIGHEST = lax.Precision.HIGHEST
 FILLS = 4
 VMEM_LIMIT = 16 * 1024 * 1024
-BIG_LIMIT = 60 * 1024 * 1024
+BIG_LIMIT = 56 * 1024 * 1024
 
 
 def tile_of(piece):
@@ -54,7 +54,9 @@
     return pl.BlockSpec(memory_space=memory_space)
 
 
-def pack_kernel(pixel_ref, space_ref, x_ref, out_ref, cand_ref, held, in_sems, out_sems):
+def pack_kernel(
+    pixel_ref, space_ref, x_ref, out_ref, cand_ref, held, pieces, in_sems, out_sems
+):
     step = OWN_IFGS // FILLS
     fills, sends = [], []
     for i in range(FILLS):
@@ -62,19 +64,18 @@
         fills.append(
             pltpu.make_async_copy(x_ref.at[ifgs], held.at[ifgs], in_sems.at[i])
         )
-        fills[-1].start()
+        sends.append(
+            pltpu.make_async_copy(pieces.at[i], out_ref.at[:, ifgs], out_sems.at[i])
+        )
+    fills[0].start()
     for i in range(FILLS):
-        ifgs = pl.ds(i * step, step)
         fills[i].wait()
+        if i + 1 < FILLS:
+            fills[i + 1].start()
         for piece in range(STACK):
             r, c = tile_of(piece)
-            send = pltpu.make_async_copy(
-                held.at[ifgs, pl.ds(r, SUB), pl.ds(c, LANE)],
-                out_ref.at[piece, ifgs],
-                out_sems.at[i, piece],
-            )
-            send.start()
-            sends.append(send)
+            pieces[i, piece] = held[i * step : (i + 1) * step, r : r + SUB, c : c + LANE]
+        sends[i].start()
     flat = pixel_ref[0]
     row = flat // (SPACE * COLS)
     col = lax.rem(flat, COLS)
@@ -99,16 +100,18 @@
         send.wait()
 
 
-def operator_kernel(pairs_ref, design_ref, design_t_ref, op_ref):
+def design_kernel(pairs_ref, design_t_ref):
     dates = iota((DATES, IFGS), 0)
     later = (pairs_ref[1:2, :] == dates).astype(F32)
     earlier = (pairs_ref[0:1, :] == dates).astype(F32)
     design_t = later - earlier
     design_t_ref[...] = design_t.astype(BF16)
-    design_ref[...] = jnp.concatenate([design_t.T] * 2, axis=1).astype(BF16)
+
+
+def operator_kernel(design_t_ref, op_ref):
     normal = lax.dot_general(
-        design_t.astype(BF16),
-        design_t.astype(BF16),
+        design_t_ref[...],
+        design_t_ref[...],
         (((1,), (1,)), ((), ())),
         preferred_element_type=F32,
     )
@@ -117,7 +120,7 @@
     diag = jnp.sum(normal * eye, axis=0, keepdims=True)
     error = eye - normal / diag
     inverse = eye / diag
-    bound = 14.0 * jnp.max(diag)
+    bound = 7.0 * jnp.max(diag)
     mul = functools.partial(jnp.dot, precision=HIGHEST, preferred_element_type=F32)
 
     def step(carry):
@@ -140,8 +143,25 @@
     op_ref[...] = jnp.concatenate([first, second, first], axis=1)
 
 
+def moment_kernel(x_ref, design_t_ref, moment_ref):
+    dot = functools.partial(jnp.dot, preferred_element_type=F32)
+    for first in range(0, SUB, WIDE // LANE):
+        rows = range(first, first + WIDE // LANE)
+        part = slice(first * LANE, first * LANE + WIDE)
+        x = jnp.concatenate([x_ref[pl.ds(r, IFGS, stride=SUB), :] for r in rows], axis=1)
+        moment_ref[:, part] = sum(dot(design_t_ref[...], term) for term in split2(x))
+
+
 def invert_kernel(
-    place_ref, x_ref, refs_ref, design_ref, design_t_ref, op_ref, mask_ref, high_ref, sums_ref
+    place_ref,
+    x_ref,
+    moment_ref,
+    refs_ref,
+    design_t_ref,
+    op_ref,
+    mask_ref,
+    high_ref,
+    sums_ref,
 ):
     place = place_ref[0]
     row_tile = pl.multiple_of((place // 8) * SUB, SUB)
@@ -155,16 +175,21 @@
     ifg = iota((IFGS, LANE), 0)
     own = iota((IFGS, LANE), 1) == ifg - ((ifg * 1821) >> 16) * OWN_IFGS
     ref_phase = jnp.sum(jnp.where(own, refs, 0.0), axis=1, keepdims=True)
-    rows_at_once = WIDE // LANE
     dot = functools.partial(jnp.dot, preferred_element_type=F32)
+    design = design_t_ref[...].astype(F32).T
+    design = jnp.concatenate([design, design], axis=1).astype(BF16)
+    ref_columns = jnp.broadcast_to(ref_phase, (IFGS, LANE))
+    ref_moment = sum(dot(design_t_ref[...], term) for term in split2(ref_columns))
+    ref_moment = jnp.concatenate([ref_moment] * (WIDE // LANE), axis=1)
     sums = jnp.zeros((OUT_ROWS, LANE), F32)
-    for first in range(0, SUB, rows_at_once):
-        rows = range(first, first + rows_at_once)
+    for first in range(0, SUB, WIDE // LANE):
+        rows = range(first, first + WIDE // LANE)
+        columns = slice(first * LANE, first * LANE + WIDE)
         x = jnp.concatenate([x_ref[pl.ds(r, IFGS, stride=SUB), :] for r in rows], axis=1)
         x = x - ref_phase
-        moment, moment_rest = split2(sum(dot(design_t_ref[...], term) for term in split2(x)))
+        moment, moment_rest = split2(moment_ref[:, columns] - ref_moment)
         both = dot(op_ref[...], jnp.concatenate([moment, moment, moment_rest], axis=0))
-        model = dot(design_ref[...], jnp.concatenate(split2(both[:DATES]), axis=0))
+        model = dot(design, jnp.concatenate(split2(both[:DATES]), axis=0))
         gap = x - model
         misfit = jnp.sum(gap * gap, axis=0, keepdims=True) * (1.0 / IFGS)
         for i, r in enumerate(rows):
@@ -260,38 +285,51 @@
         (full(pltpu.HBM), full()),
         [
             pltpu.VMEM((OWN_IFGS, ROWS, COLS), F32),
+            pltpu.VMEM((FILLS, STACK, OWN_IFGS // FILLS, SUB, LANE), F32),
             pltpu.SemaphoreType.DMA((FILLS,)),
-            pltpu.SemaphoreType.DMA((FILLS, STACK)),
+            pltpu.SemaphoreType.DMA((FILLS,)),
         ],
         nbytes=2 * 4 * OWN_IFGS * ROWS * COLS,
         vmem=BIG_LIMIT,
     )(ref_pixel, lax.axis_index(SPACE_AXES).reshape(1), phases)
     block = lax.all_to_all(send, STACK_AXES, split_axis=0, concat_axis=0, tiled=True)
 
-    design, design_t, operator = call(
-        operator_kernel,
-        (
-            struct(IFGS, 2 * DATES, dtype=BF16),
-            struct(DATES, IFGS, dtype=BF16),
-            struct(DATES + OUT_ROWS, 3 * DATES, dtype=BF16),
-        ),
+    design_t = call(
+        design_kernel,
+        struct(DATES, IFGS, dtype=BF16),
         [full()],
-        (full(), full(), full()),
-        flops=30 * 6 * 2 * 256**3,
-        nbytes=10**6,
+        full(),
+        flops=10**4,
+        nbytes=10**4,
     )(pairs.T)
 
     refs = cand
     for axis in ("z_lo", "z_hi"):
         refs = jnp.sum(lax.all_gather(refs, axis, axis=0, tiled=True), axis=0, keepdims=True)
-    refs, block, operator = lax.optimization_barrier((refs, block, operator))
+    refs = jnp.broadcast_to(refs, (2 * STACK, LANE))
+    refs, block, design_t = lax.optimization_barrier((refs, block, design_t))
     refs = lax.all_to_all(
-        jnp.broadcast_to(refs, (2 * STACK, LANE)),
-        ("x_hi",) + STACK_AXES,
-        split_axis=0,
-        concat_axis=0,
-        tiled=True,
-    )
+        refs, ("x_hi",) + STACK_AXES, split_axis=0, concat_axis=0, tiled=True
+    )
+
+    operator = call(
+        operator_kernel,
+        struct(DATES + OUT_ROWS, 3 * DATES, dtype=BF16),
+        [full()],
+        full(),
+        flops=10**4,
+        nbytes=10**4,
+    )(design_t)
+
+    flat = block.reshape(IFGS * SUB, LANE)
+    moment = call(
+        moment_kernel,
+        struct(DATES, PIXELS),
+        [full()] * 2,
+        full(),
+        flops=10**4,
+        nbytes=10**4,
+    )(flat, design_t)
 
     high, sums = call(
         invert_kernel,
@@ -302,9 +340,9 @@
         nbytes=4 * (IFGS + OUT_ROWS) * PIXELS,
     )(
         lax.axis_index(STACK_AXES).reshape(1),
-        block.reshape(IFGS * SUB, LANE),
+        flat,
+        moment,
         refs,
-        design,
         design_t,
         operator,
         coherent,

time: 92 us -> 96.7 us (1.051)
  waiting for transfers between devices: 5.48 us -> 0.01 us
  blocking collectives: 56.1 us -> 60.5 us
  Pallas kernels: 13.9 us -> 17.2 us
  starting transfers between devices: 13.7 us -> 15.1 us
    all_to_all x1, waiting for transfers between devices: 5.47 us -> 0.01 us  [body(): lax.all_to_all(refs, ('x_hi',) + STACK_AXES, split_axis=0, concat_axis=0,...]
    all_to_all x1, blocking collectives: 26.2 us -> 30.6 us  [body(): lax.all_to_all(pieces.reshape(STACK, PIECE, SUB, LANE), STACK_AXES, split...]
    pallas_call x1, Pallas kernels: 3.6 us -> 6.39 us  [body(): call(pack_kernel, (struct(STACK, OWN_IFGS, SUB, LANE), struct(1, LANE)),...]
    all_to_all x1, starting transfers between devices: 7.09 us -> 8.47 us  [body(): lax.all_to_all(refs, ('x_hi',) + STACK_AXES, split_axis=0, concat_axis=0,...]
    pallas_call x1 -> x3, Pallas kernels: 5.31 us -> 5.71 us  [the longest x1 4.83 us: body(): call(operator_kernel, struct(DATES + OUT_ROWS, 3 * DATES, dtype=BF16), [f...]
  transfers between devices with their start and end apart: 3 -> 3, of which waited for: 1 -> 0; matrix products, arithmetic and copies ran while one was open for 0% -> 0% of each run, Pallas kernels for 6% -> 6%
where the time goes in v2:
time: 96.7 us; the launch traced here: 95.7 us
  blocking collectives  60.5 us (63%)
  Pallas kernels  17.2 us (18%)
  starting transfers between devices  15.1 us (16%)
  local copies, waits for them, and re-layouts  1.46 us (2%)
  between operations  1.41 us (1%)
    all_to_all x1, blocking collectives, body(): lax.all_to_all(pieces.reshape(STACK, PIECE, SUB, LANE), STACK_AXES, split...  30.6 us
    all_gather x2, blocking collectives, body(): lax.all_gather(refs, axis, axis=0, tiled=True)  29.9 us
    all_to_all x1, starting transfers between devices, body(): lax.all_to_all(refs, ('x_hi',) + STACK_AXES, split_axis=0, concat_axis=0,...  8.47 us
    pallas_call x1, Pallas kernels, body(): call(pack_kernel, (struct(STACK, OWN_IFGS, SUB, LANE), struct(1, LANE)),...  6.39 us
    all_to_all x1, starting transfers between devices, body(): lax.all_to_all(send, STACK_AXES, split_axis=0, concat_axis=0, tiled=True)  5.96 us
    pallas_call x1, Pallas kernels, body(): call(operator_kernel, struct(DATES + OUT_ROWS, 3 * DATES, dtype=BF16), [f...  4.83 us
    pallas_call x1, Pallas kernels, body(): call(invert_kernel, (struct(OUT_ROWS, PIXELS), struct(OUT_ROWS, LANE)), [...  3.67 us
  transfers between devices with their start and end apart: 3, of which 0 were waited for; matrix products, arithmetic and copies ran while one was open for 0% of the time, Pallas kernels for 6%

profile of v2, /device:TPU:6, one launch (start us, length us, event | category | flops | bytes accessed | tf_op | source)
XLA Modules:
  0.0 95.7 jit_solution(7896752515716909049)
XLA Ops:
  1.3 6.4 %shard_map.59 = (f32[16,36,8,128]{3,2,1,0:T(8,128)}, f32[1,128]{1,0:T(1,128)}) custom-call(s32[1]{0:T(128)S(6)} %copy.6.pixel_ref, s32[1]{0:T(128)} %bitcast.1.space_ref, f32[36,16,1024]{2,1,0:T(8,128)} %x_ref.1), custom_call_target="tpu_custom_call" | custom-call | bytes 4718592 | tf_op jit(solution)/shard_map/pallas_call | solution.py:281
  7.7 0.0 copy-start.1
  7.7 0.0 copy-start.2
  7.7 6.0 %all-to-all-start = ((f32[16,36,8,128]{3,2,1,0:T(8,128)}), f32[16,36,8,128]{3,2,1,0:T(8,128)S(1)}, u32[]{:S(2)}, u32[]{:S(2)}) async-start(f32[16,36,8,128]{3,2,1,0:T(8,128)} %get-tuple-element.10), calls=%async_computation | async-start | bytes 4718592 | tf_op jit(solution)/shard_map/all_to_all | solution.py:295
  13.7 0.0 copy-done.1
  13.7 0.1 shard_map.60.design_t_ref
  13.7 0.0 copy-done.2
  13.8 12.1 %all-gather.1 = f32[4,1,128]{2,1,0:T(1,128)S(1)} all-gather(f32[1,1,128]{2,1,0:T(1,128)S(1)} %bitcast.14), channel_id=1, replica_groups=mesh['y'=4,'x_lo'=2,'core'=2,'x_hi'=2,'z_hi'=4,'z_lo'=4] {'z_lo'}, dimensions={0}, use_global_device_ids=true | all-gather | bytes 2560 | tf_op jit(solution)/shard_map/all_gather | solution.py:308
  25.9 17.7 %all-gather.2 = f32[4,1,128]{2,1,0:T(1,128)S(1)} all-gather(f32[1,1,128]{2,1,0:T(1,128)S(1)} %bitcast.13), channel_id=2, replica_groups=mesh['y'=4,'x_lo'=2,'core'=2,'x_hi'=2,'z_hi'=4,'z_lo'=4] {'z_hi'}, dimensions={0}, use_global_device_ids=true | all-gather | bytes 2560 | tf_op jit(solution)/shard_map/all_gather | solution.py:308
  43.7 0.0 all-to-all-done
  43.7 0.6 broadcast_in_dim.10
  44.3 8.5 %all-to-all-start.1 = ((f32[32,1,128]{2,1,0:T(1,128)}), f32[32,1,128]{2,1,0:T(1,128)}, u32[]{:S(2)}, u32[]{:S(2)}) async-start(f32[32,1,128]{2,1,0:T(1,128)} %bitcast.6), calls=%async_computation.1 | async-start | bytes 32768 | tf_op jit(solution)/shard_map/all_to_all | solution.py:311
  52.8 4.8 %shard_map.62.op_ref = bf16[400,432]{1,0:T(8,128)(2,1)S(1)} custom-call(bf16[144,576]{1,0:T(8,128)(2,1)S(1)} %shard_map.60.design_t_ref), custom_call_target="tpu_custom_call" | custom-call | flops 10000 | bytes 10000 | tf_op jit(solution)/shard_map/pallas_call | solution.py:315
  57.6 0.8 shard_map.61.moment_ref
  58.4 0.0 all-to-all-done.1
  58.4 0.0 copy-start
  58.4 0.8 copy-done
  59.3 3.7 %shard_map.63 = (f32[256,1024]{1,0:T(8,128)S(1)}, f32[256,128]{1,0:T(8,128)S(1)}) custom-call(s32[1]{0:T(128)} %bitcast.place_ref, f32[4608,128]{1,0:T(8,128)S(1)} %bitcast.10, f32[144,1024]{1,0:T(8,128)S(1)} %shard_map.61.moment_ref, f32[32,128]{1,0:T(8,128)} %bitcast.7.refs_ref, bf16[144,576]{1,0:T(8,128)(2,1)S(1)} %shard_map.60.design_t_ref, ...), custom_call_target="tpu_custom_call" | custom-call | flops 2123366400 | bytes 3407872 | tf_op jit(solution)/shard_map/pallas_call | solution.py:334
  62.9 0.7 collective-permute-start
  63.6 0.0 collective-permute-done.sums_ref
  63.6 0.2 shard_map.64
  63.8 30.6 %all_to_all.21.x_ref = f32[16,12,8,128]{3,2,1,0:T(8,128)S(1)} all-to-all(f32[16,12,8,128]{3,2,1,0:T(8,128)S(1)} %bitcast.11), channel_id=1, replica_groups=mesh['y'=4,'x_lo'=2,'core'=2,'x_hi'=2,'z_hi'=4,'z_lo'=4] {'y','x_lo','co..., dimensions={0} | all-to-all | bytes 1572864 | tf_op jit(solution)/shard_map/all_to_all | solution.py:371
  94.5 1.2 %shard_map.65 = (f32[9,1024]{1,0:T(8,128)}, f32[9,16,1024]{2,1,0:T(8,128)}) custom-call(f32[16,12,8,128]{3,2,1,0:T(8,128)S(1)} %all_to_all.21.x_ref, s32[16,1024]{1,0:T(8,128)S(1)} %copy-done), custom_call_target="tpu_custom_call" | custom-call | flops 75497472 | bytes 1572864 | tf_op jit(solution)/shard_map/pallas_call | solution.py:375
  (2 shorter events, 0.0 us)
Async XLA Ops:
  7.7 6.0 %copy-start.1 = (s32[576,2]{0,1:T(2,128)S(1)}, s32[576,2]{0,1:T(2,128)}, u32[]{:S(2)}) copy-start(s32[576,2]{0,1:T(2,128)} %param.5) | copy-start | bytes 13828
  7.7 6.1 %copy-start.2 = (f32[1,128]{1,0:T(1,128)S(1)}, f32[1,128]{1,0:T(1,128)}, u32[]{:S(2)}) copy-start(f32[1,128]{1,0:T(1,128)} %get-tuple-element.9) | copy-start | bytes 1540
  7.7 36.0 %all-to-all-start = ((f32[16,36,8,128]{3,2,1,0:T(8,128)}), f32[16,36,8,128]{3,2,1,0:T(8,128)S(1)}, u32[]{:S(2)}, u32[]{:S(2)}) async-start(f32[16,36,8,128]{3,2,1,0:T(8,128)} %get-tuple-element.10), calls=%async_computation | async-start | bytes 4718592 | tf_op jit(solution)/shard_map/all_to_all | solution.py:295
  44.3 14.1 %all-to-all-start.1 = ((f32[32,1,128]{2,1,0:T(1,128)}), f32[32,1,128]{2,1,0:T(1,128)}, u32[]{:S(2)}, u32[]{:S(2)}) async-start(f32[32,1,128]{2,1,0:T(1,128)} %bitcast.6), calls=%async_computation.1 | async-start | bytes 32768 | tf_op jit(solution)/shard_map/all_to_all | solution.py:311
  58.4 0.8 copy-start
  62.9 0.7 collective-permute-start

commit v3 on v1

--- a/solution.py
+++ b/solution.py
@@ -24,7 +24,7 @@
 SUMS = OWN_DATES + 1
 PIECE = SUMS + GROUP // SUB
 PIXELS = SUB * LANE
-WIDE = 256
+WIDE = 512
 
 STACK_AXES = ("y", "x_lo", "core")
 SPACE_AXES = ("x_hi", "z_hi", "z_lo")
@@ -32,8 +32,7 @@
 F32 = jnp.float32
 BF16 = jnp.bfloat16
 HIGHEST = lax.Precision.HIGHEST
-FILLS = 4
-VMEM_LIMIT = 16 * 1024 * 1024
+VMEM_LIMIT = 24 * 1024 * 1024
 BIG_LIMIT = 60 * 1024 * 1024
 
 
@@ -46,6 +45,12 @@
     return first, (value - first.astype(F32)).astype(BF16)
 
 
+def split3(value):
+    first, rest = split2(value)
+    third = value - first.astype(F32) - rest.astype(F32)
+    return first, rest, third.astype(BF16)
+
+
 def iota(shape, axis):
     return lax.broadcasted_iota(jnp.int32, shape, axis)
 
@@ -55,33 +60,26 @@
 
 
 def pack_kernel(pixel_ref, space_ref, x_ref, out_ref, cand_ref, held, in_sems, out_sems):
-    step = OWN_IFGS // FILLS
     fills, sends = [], []
-    for i in range(FILLS):
-        ifgs = pl.ds(i * step, step)
+    for piece in range(STACK):
+        r, c = tile_of(piece)
         fills.append(
-            pltpu.make_async_copy(x_ref.at[ifgs], held.at[ifgs], in_sems.at[i])
+            pltpu.make_async_copy(
+                x_ref.at[:, pl.ds(r, SUB), pl.ds(c, LANE)], held.at[piece], in_sems.at[piece]
+            )
+        )
+        sends.append(
+            pltpu.make_async_copy(held.at[piece], out_ref.at[piece], out_sems.at[piece])
         )
         fills[-1].start()
-    for i in range(FILLS):
-        ifgs = pl.ds(i * step, step)
-        fills[i].wait()
-        for piece in range(STACK):
-            r, c = tile_of(piece)
-            send = pltpu.make_async_copy(
-                held.at[ifgs, pl.ds(r, SUB), pl.ds(c, LANE)],
-                out_ref.at[piece, ifgs],
-                out_sems.at[i, piece],
-            )
-            send.start()
-            sends.append(send)
+    for fill, send in zip(fills, sends):
+        fill.wait()
+        send.start()
     flat = pixel_ref[0]
     row = flat // (SPACE * COLS)
     col = lax.rem(flat, COLS)
-    row_tile = pl.multiple_of((row // SUB) * SUB, SUB)
-    col_tile = pl.multiple_of((col // LANE) * LANE, LANE)
     is_owner = space_ref[0] == lax.rem(flat, SPACE * COLS) // COLS
-    picked = held[:, pl.ds(row_tile, SUB), pl.ds(col_tile, LANE)]
+    picked = held[(row // SUB) * (COLS // LANE) + col // LANE]
     shape = (OWN_IFGS, SUB, LANE)
     here = (iota(shape, 1) == lax.rem(row, SUB)) & (iota(shape, 2) == lax.rem(col, LANE))
     here = here & is_owner
@@ -97,6 +95,11 @@
     cand_ref[...] = rows[:1]
     for send in sends:
         send.wait()
+
+
+def rows_kernel(parts_ref, rows_ref):
+    total = jnp.sum(parts_ref[...], axis=0, keepdims=True)
+    rows_ref[...] = jnp.broadcast_to(total, rows_ref.shape)
 
 
 def operator_kernel(pairs_ref, design_ref, design_t_ref, op_ref):
@@ -117,7 +120,7 @@
     diag = jnp.sum(normal * eye, axis=0, keepdims=True)
     error = eye - normal / diag
     inverse = eye / diag
-    bound = 14.0 * jnp.max(diag)
+    bound = 7.0 * jnp.max(diag)
     mul = functools.partial(jnp.dot, precision=HIGHEST, preferred_element_type=F32)
 
     def step(carry):
@@ -128,15 +131,15 @@
         lambda carry: carry[0] < bound, step, (jnp.float32(1.0), inverse, error)
     )
     inverse = inverse + mul(inverse, eye - mul(normal, inverse))
-    steps = iota((DATES, DATES), 0) - iota((DATES, DATES), 1)
+    out_row = iota((OUT_ROWS, DATES), 0)
+    place = out_row & (GROUP - 1)
+    date = (out_row >> 4) * OWN_DATES + place
+    steps = date - iota((OUT_ROWS, DATES), 1)
     gauss = jnp.exp(-(steps * steps).astype(F32) / (2.0 * TAU * TAU))
     smooth = gauss / jnp.sum(gauss, axis=1, keepdims=True)
-    high = mul(eye - smooth, inverse)
-    out_row = iota((OUT_ROWS, DATES), 0)
-    place = out_row & (GROUP - 1)
-    date = jnp.where(place < OWN_DATES, (out_row >> 4) * OWN_DATES + place, -1)
-    spread = (iota((OUT_ROWS, DATES), 1) == date).astype(F32)
-    first, second = split2(jnp.concatenate([inverse, mul(spread, high)], axis=0))
+    keep = (steps == 0).astype(F32) - smooth
+    high = mul(jnp.where(place < OWN_DATES, keep, 0.0), inverse)
+    first, second = split2(jnp.concatenate([inverse, high], axis=0))
     op_ref[...] = jnp.concatenate([first, second, first], axis=1)
 
 
@@ -150,8 +153,11 @@
     is_weight = (iota((OUT_ROWS, LANE), 0) & (GROUP - 1)) == OWN_DATES
     ifg = iota((IFGS, STACK), 0)
     spread = (iota((IFGS, STACK), 1) == (ifg * 1821) >> 16).astype(F32)
+    spread = jnp.concatenate([spread] * 3, axis=1).astype(BF16)
     refs = refs_ref[:STACK] + refs_ref[STACK:]
-    refs = jnp.dot(spread, refs, precision=HIGHEST, preferred_element_type=F32)
+    refs = jnp.dot(
+        spread, jnp.concatenate(split3(refs), axis=0), preferred_element_type=F32
+    )
     ifg = iota((IFGS, LANE), 0)
     own = iota((IFGS, LANE), 1) == ifg - ((ifg * 1821) >> 16) * OWN_IFGS
     ref_phase = jnp.sum(jnp.where(own, refs, 0.0), axis=1, keepdims=True)
@@ -175,7 +181,8 @@
             sums = sums + weighted
             high = jnp.where(is_weight, weighted, high)
             high_ref[:, r * LANE : (r + 1) * LANE] = high
-    sums_ref[...] = sums
+    for t in range(STACK):
+        sums_ref[t * SUMS : (t + 1) * SUMS] = sums[t * GROUP : t * GROUP + SUMS]
 
 
 def pieces_kernel(high_ref, sums_ref, out_ref):
@@ -186,7 +193,9 @@
             ]
     for t in range(STACK):
         last = t * PIECE * SUB + SUMS * SUB
-        out_ref[last : last + GROUP] = sums_ref[t * GROUP : (t + 1) * GROUP]
+        sums = sums_ref[t * SUMS : (t + 1) * SUMS]
+        pad = jnp.zeros((GROUP - SUMS, LANE), F32)
+        out_ref[last : last + GROUP] = jnp.concatenate([sums, pad], axis=0)
 
 
 def screen_kernel(x_ref, mask_ref, screens_ref, residual_ref):
@@ -259,9 +268,9 @@
         [full(pltpu.SMEM), full(pltpu.SMEM), full(pltpu.HBM)],
         (full(pltpu.HBM), full()),
         [
-            pltpu.VMEM((OWN_IFGS, ROWS, COLS), F32),
-            pltpu.SemaphoreType.DMA((FILLS,)),
-            pltpu.SemaphoreType.DMA((FILLS, STACK)),
+            pltpu.VMEM((STACK, OWN_IFGS, SUB, LANE), F32),
+            pltpu.SemaphoreType.DMA((STACK,)),
+            pltpu.SemaphoreType.DMA((STACK,)),
         ],
         nbytes=2 * 4 * OWN_IFGS * ROWS * COLS,
         vmem=BIG_LIMIT,
@@ -281,12 +290,13 @@
         nbytes=10**6,
     )(pairs.T)
 
-    refs = cand
-    for axis in ("z_lo", "z_hi"):
-        refs = jnp.sum(lax.all_gather(refs, axis, axis=0, tiled=True), axis=0, keepdims=True)
+    refs = lax.all_gather(cand, "z_lo", axis=0, tiled=True)
+    refs = jnp.sum(refs, axis=0, keepdims=True)
+    refs = lax.all_gather(refs, "z_hi", axis=0, tiled=True)
+    refs = call(rows_kernel, struct(2 * STACK, LANE), [full()], full())(refs)
     refs, block, operator = lax.optimization_barrier((refs, block, operator))
     refs = lax.all_to_all(
-        jnp.broadcast_to(refs, (2 * STACK, LANE)),
+        refs,
         ("x_hi",) + STACK_AXES,
         split_axis=0,
         concat_axis=0,
@@ -295,7 +305,7 @@
 
     high, sums = call(
         invert_kernel,
-        (struct(OUT_ROWS, PIXELS), struct(OUT_ROWS, LANE)),
+        (struct(OUT_ROWS, PIXELS), struct(STACK * SUMS, LANE)),
         [full(pltpu.SMEM)] + [full()] * 6,
         (full(), full()),
         flops=6 * 2 * PIXELS * DATES * 1200,

time: 92 us -> 89.3 us (0.971)
  Pallas kernels: 13.9 us -> 12.6 us
    pallas_call x1 -> x2, Pallas kernels: 3.55 us -> 3.48 us  [the longest x1 2.86 us: body(): call(invert_kernel, (struct(OUT_ROWS, PIXELS), struct(STACK * SUMS, LANE)...]
where the time goes in v3:
time: 89.3 us; the launch traced here: 88.5 us
  blocking collectives  55.3 us (62%)
  starting transfers between devices  13.7 us (15%)
  Pallas kernels  12.6 us (14%)
  waiting for transfers between devices  5.48 us (6%)
  between operations  1.38 us (2%)
    all_to_all x1, blocking collectives, body(): lax.all_to_all(pieces.reshape(STACK, PIECE, SUB, LANE), STACK_AXES, split...  25.4 us
    all_gather x1, blocking collectives, body(): refs = lax.all_gather(refs, 'z_hi', axis=0, tiled=True)  17.7 us
    all_gather x1, blocking collectives, body(): refs = lax.all_gather(cand, 'z_lo', axis=0, tiled=True)  12.1 us
    all_to_all x1, starting transfers between devices, body(): lax.all_to_all(refs, ('x_hi',) + STACK_AXES, split_axis=0, concat_axis=0,...  7.1 us
    all_to_all x1, starting transfers between devices, body(): lax.all_to_all(send, STACK_AXES, split_axis=0, concat_axis=0, tiled=True)  5.96 us
    all_to_all x1, waiting for transfers between devices, body(): lax.all_to_all(refs, ('x_hi',) + STACK_AXES, split_axis=0, concat_axis=0,...  5.47 us
    pallas_call x1, Pallas kernels, body(): call(operator_kernel, (struct(IFGS, 2 * DATES, dtype=BF16), struct(DATES,...  4.48 us
    pallas_call x1, Pallas kernels, body(): call(pack_kernel, (struct(STACK, OWN_IFGS, SUB, LANE), struct(1, LANE)),...  3.25 us
  transfers between devices with their start and end apart: 3, of which 1 were waited for; matrix products, arithmetic and copies ran while one was open for 0% of the time, Pallas kernels for 6%

profile of v3, /device:TPU:6, one launch (start us, length us, event | category | flops | bytes accessed | tf_op | source)
XLA Modules:
  0.0 88.5 jit_solution(12224130044369822297)
XLA Ops:
  1.3 3.3 %shard_map.59 = (f32[16,36,8,128]{3,2,1,0:T(8,128)}, f32[1,128]{1,0:T(1,128)}) custom-call(s32[1]{0:T(128)S(6)} %copy.8.pixel_ref, s32[1]{0:T(128)} %bitcast.1.space_ref, f32[36,16,1024]{2,1,0:T(8,128)} %x_ref.1), custom_call_target="tpu_custom_call" | custom-call | bytes 4718592 | tf_op jit(solution)/shard_map/pallas_call | solution.py:265
  4.5 0.0 copy-start.2
  4.6 0.0 copy-start.1
  4.6 6.0 %all-to-all-start = ((f32[16,36,8,128]{3,2,1,0:T(8,128)}), f32[16,36,8,128]{3,2,1,0:T(8,128)S(1)}, u32[]{:S(2)}, u32[]{:S(2)}) async-start(f32[16,36,8,128]{3,2,1,0:T(8,128)} %get-tuple-element.13), calls=%async_computation | async-start | bytes 4718592 | tf_op jit(solution)/shard_map/all_to_all | solution.py:278
  10.5 0.0 copy-done.2
  10.5 12.1 %all-gather.1 = f32[4,1,128]{2,1,0:T(1,128)S(1)} all-gather(f32[1,1,128]{2,1,0:T(1,128)S(1)} %bitcast.18), channel_id=1, replica_groups=mesh['y'=4,'x_lo'=2,'core'=2,'x_hi'=2,'z_hi'=4,'z_lo'=4] {'z_lo'}, dimensions={0}, use_global_device_ids=true | all-gather | bytes 2560 | tf_op jit(solution)/shard_map/all_gather | solution.py:293
  22.7 17.7 %all-gather.2 = f32[4,1,128]{2,1,0:T(1,128)S(1)} all-gather(f32[1,1,128]{2,1,0:T(1,128)S(1)} %bitcast.17), channel_id=2, replica_groups=mesh['y'=4,'x_lo'=2,'core'=2,'x_hi'=2,'z_hi'=4,'z_lo'=4] {'z_hi'}, dimensions={0}, use_global_device_ids=true | all-gather | bytes 2560 | tf_op jit(solution)/shard_map/all_gather | solution.py:295
  40.4 0.6 shard_map.60
  41.0 0.0 copy-done.1
  41.0 0.0 copy-start
  41.0 4.5 %shard_map.61 = (bf16[576,288]{1,0:T(8,128)(2,1)S(1)}, bf16[144,576]{1,0:T(8,128)(2,1)S(1)}, bf16[400,432]{1,0:T(8,128)(2,1)S(1)}) custom-call(s32[2,576]{1,0:T(2,128)S(1)} %bitcast.16), custom_call_target="tpu_custom_call" | custom-call | flops 6039797760 | bytes 1000000 | tf_op jit(solution)/shard_map/pallas_call | solution.py:280
  45.5 0.0 all-to-all-done
  45.5 7.1 %all-to-all-start.1 = ((f32[32,1,128]{2,1,0:T(1,128)}), f32[32,1,128]{2,1,0:T(1,128)S(1)}, u32[]{:S(2)}, u32[]{:S(2)}) async-start(f32[32,1,128]{2,1,0:T(1,128)} %bitcast.8), calls=%async_computation.1 | async-start | bytes 32768 | tf_op jit(solution)/shard_map/all_to_all | solution.py:298
  52.6 5.5 %all-to-all-done.1 = f32[32,1,128]{2,1,0:T(1,128)S(1)} async-done(((f32[32,1,128]{2,1,0:T(1,128)}), f32[32,1,128]{2,1,0:T(1,128)S(1)}, u32[]{:S(2)}, u32[]{:S(2)}) %all-to-all-start.1) | async-done | bytes 16416 | tf_op jit(solution)/shard_map/all_to_all | solution.py:298
  58.1 0.0 copy-done
  58.1 2.9 %shard_map.62 = (f32[256,1024]{1,0:T(8,128)S(1)}, f32[160,128]{1,0:T(8,128)S(1)}) custom-call(s32[1]{0:T(128)} %bitcast.place_ref, f32[4608,128]{1,0:T(8,128)S(1)} %bitcast.13, f32[32,128]{1,0:T(8,128)S(1)} %bitcast.14, bf16[576,288]{1,0:T(8,128)(2,1)S(1)} %get-tuple-element.17.design_ref, bf16[144,576]{1,0:T(8,128)(2,1)S(1)} %get-tuple-element.18.design_t_ref, ...), custom_call_target="tpu_custom_call" | custom-call | flops 2123366400 | bytes 3407872 | tf_op jit(solution)/shard_map/pallas_call | solution.py:306
  61.0 0.7 collective-permute-start
  61.7 0.0 collective-permute-done.sums_ref
  61.7 0.2 shard_map.63
  61.9 25.4 %all_to_all.21.x_ref = f32[16,12,8,128]{3,2,1,0:T(8,128)S(1)} all-to-all(f32[16,12,8,128]{3,2,1,0:T(8,128)S(1)} %bitcast.12), channel_id=1, replica_groups=mesh['y'=4,'x_lo'=2,'core'=2,'x_hi'=2,'z_hi'=4,'z_lo'=4] {'y','x_lo','co..., dimensions={0} | all-to-all | bytes 1572864 | tf_op jit(solution)/shard_map/all_to_all | solution.py:343
  87.3 1.2 %shard_map.64 = (f32[9,1024]{1,0:T(8,128)}, f32[9,16,1024]{2,1,0:T(8,128)}) custom-call(f32[16,12,8,128]{3,2,1,0:T(8,128)S(1)} %all_to_all.21.x_ref, s32[16,1024]{1,0:T(8,128)S(1)} %copy-done), custom_call_target="tpu_custom_call" | custom-call | flops 75497472 | bytes 1572864 | tf_op jit(solution)/shard_map/pallas_call | solution.py:347
  (1 shorter events, 0.0 us)
Async XLA Ops:
  4.5 6.0 %copy-start.2 = (f32[1,128]{1,0:T(1,128)S(1)}, f32[1,128]{1,0:T(1,128)}, u32[]{:S(2)}) copy-start(f32[1,128]{1,0:T(1,128)} %get-tuple-element.12) | copy-start | bytes 1540
  4.6 36.5 %copy-start.1 = (s32[576,2]{0,1:T(2,128)S(1)}, s32[576,2]{0,1:T(2,128)}, u32[]{:S(2)}) copy-start(s32[576,2]{0,1:T(2,128)} %param.5) | copy-start | bytes 13828
  4.6 40.9 %all-to-all-start = ((f32[16,36,8,128]{3,2,1,0:T(8,128)}), f32[16,36,8,128]{3,2,1,0:T(8,128)S(1)}, u32[]{:S(2)}, u32[]{:S(2)}) async-start(f32[16,36,8,128]{3,2,1,0:T(8,128)} %get-tuple-element.13), calls=%async_computation | async-start | bytes 4718592 | tf_op jit(solution)/shard_map/all_to_all | solution.py:278
  41.0 17.1 %copy-start = (s32[16,1024]{1,0:T(8,128)S(1)}, s32[16,1024]{1,0:T(8,128)}, u32[]{:S(2)}) copy-start(s32[16,1024]{1,0:T(8,128)} %mask_ref.3) | copy-start | bytes 196612
  45.5 12.6 %all-to-all-start.1 = ((f32[32,1,128]{2,1,0:T(1,128)}), f32[32,1,128]{2,1,0:T(1,128)S(1)}, u32[]{:S(2)}, u32[]{:S(2)}) async-start(f32[32,1,128]{2,1,0:T(1,128)} %bitcast.8), calls=%async_computation.1 | async-start | bytes 32768 | tf_op jit(solution)/shard_map/all_to_all | solution.py:298
  61.0 0.7 collective-permute-start

commit v4 on v3

--- a/solution.py
+++ b/solution.py
@@ -102,16 +102,22 @@
     rows_ref[...] = jnp.broadcast_to(total, rows_ref.shape)
 
 
-def operator_kernel(pairs_ref, design_ref, design_t_ref, op_ref):
+def design_kernel(pairs_ref, design_t_ref):
     dates = iota((DATES, IFGS), 0)
     later = (pairs_ref[1:2, :] == dates).astype(F32)
     earlier = (pairs_ref[0:1, :] == dates).astype(F32)
     design_t = later - earlier
     design_t_ref[...] = design_t.astype(BF16)
-    design_ref[...] = jnp.concatenate([design_t.T] * 2, axis=1).astype(BF16)
+
+
+def operator_kernel(design_t_ref, op_ref):
+    design = design_t_ref[...].astype(F32).T
+    design = jnp.concatenate([design, design, jnp.zeros_like(design)], axis=1)
+    op_ref[DATES + OUT_ROWS :] = design.astype(BF16)
+    design_t = design_t_ref[...]
     normal = lax.dot_general(
-        design_t.astype(BF16),
-        design_t.astype(BF16),
+        design_t,
+        design_t,
         (((1,), (1,)), ((), ())),
         preferred_element_type=F32,
     )
@@ -140,21 +146,25 @@
     keep = (steps == 0).astype(F32) - smooth
     high = mul(jnp.where(place < OWN_DATES, keep, 0.0), inverse)
     first, second = split2(jnp.concatenate([inverse, high], axis=0))
-    op_ref[...] = jnp.concatenate([first, second, first], axis=1)
-
-
-def invert_kernel(
-    place_ref, x_ref, refs_ref, design_ref, design_t_ref, op_ref, mask_ref, high_ref, sums_ref
-):
+    op_ref[: DATES + OUT_ROWS] = jnp.concatenate([first, second, first], axis=1)
+
+
+def mask_kernel(place_ref, mask_ref, tile_ref):
     place = place_ref[0]
     row_tile = pl.multiple_of((place // 8) * SUB, SUB)
     col_tile = pl.multiple_of(lax.rem(place, 8) * LANE, LANE)
-    coherent = mask_ref[pl.ds(row_tile, SUB), pl.ds(col_tile, LANE)].astype(F32)
+    tile_ref[...] = mask_ref[pl.ds(row_tile, SUB), pl.ds(col_tile, LANE)].astype(F32)
+
+
+def invert_kernel(
+    x_ref, refs_ref, design_t_ref, op_ref, mask_ref, high_ref, sums_ref
+):
+    coherent = mask_ref[...]
     is_weight = (iota((OUT_ROWS, LANE), 0) & (GROUP - 1)) == OWN_DATES
     ifg = iota((IFGS, STACK), 0)
     spread = (iota((IFGS, STACK), 1) == (ifg * 1821) >> 16).astype(F32)
     spread = jnp.concatenate([spread] * 3, axis=1).astype(BF16)
-    refs = refs_ref[:STACK] + refs_ref[STACK:]
+    refs = refs_ref[...]
     refs = jnp.dot(
         spread, jnp.concatenate(split3(refs), axis=0), preferred_element_type=F32
     )
@@ -163,14 +173,17 @@
     ref_phase = jnp.sum(jnp.where(own, refs, 0.0), axis=1, keepdims=True)
     rows_at_once = WIDE // LANE
     dot = functools.partial(jnp.dot, preferred_element_type=F32)
+    design = op_ref[DATES + OUT_ROWS :, : 2 * DATES]
     sums = jnp.zeros((OUT_ROWS, LANE), F32)
     for first in range(0, SUB, rows_at_once):
         rows = range(first, first + rows_at_once)
         x = jnp.concatenate([x_ref[pl.ds(r, IFGS, stride=SUB), :] for r in rows], axis=1)
         x = x - ref_phase
         moment, moment_rest = split2(sum(dot(design_t_ref[...], term) for term in split2(x)))
-        both = dot(op_ref[...], jnp.concatenate([moment, moment, moment_rest], axis=0))
-        model = dot(design_ref[...], jnp.concatenate(split2(both[:DATES]), axis=0))
+        both = dot(
+            op_ref[: DATES + OUT_ROWS], jnp.concatenate([moment, moment, moment_rest], axis=0)
+        )
+        model = dot(design, jnp.concatenate(split2(both[:DATES]), axis=0))
         gap = x - model
         misfit = jnp.sum(gap * gap, axis=0, keepdims=True) * (1.0 / IFGS)
         for i, r in enumerate(rows):
@@ -277,47 +290,50 @@
     )(ref_pixel, lax.axis_index(SPACE_AXES).reshape(1), phases)
     block = lax.all_to_all(send, STACK_AXES, split_axis=0, concat_axis=0, tiled=True)
 
-    design, design_t, operator = call(
+    design_t = call(
+        design_kernel,
+        struct(DATES, IFGS, dtype=BF16),
+        [full()],
+        full(),
+        flops=10**4,
+        nbytes=10**4,
+    )(pairs.T)
+
+    refs = cand
+    for axis in ("z_lo", "z_hi"):
+        refs = jnp.sum(lax.all_gather(refs, axis, axis=0, tiled=True), axis=0, keepdims=True)
+    refs = lax.all_gather(refs, "x_hi", axis=0, tiled=True)
+    refs = call(rows_kernel, struct(STACK, LANE), [full()], full())(refs)
+    mask_tile = call(
+        mask_kernel, struct(SUB, LANE), [full(pltpu.SMEM), full()], full()
+    )(lax.axis_index(STACK_AXES).reshape(1), coherent)
+    refs, block, design_t, mask_tile = lax.optimization_barrier(
+        (refs, block, design_t, mask_tile)
+    )
+    refs = lax.all_to_all(refs, STACK_AXES, split_axis=0, concat_axis=0, tiled=True)
+
+    operator = call(
         operator_kernel,
-        (
-            struct(IFGS, 2 * DATES, dtype=BF16),
-            struct(DATES, IFGS, dtype=BF16),
-            struct(DATES + OUT_ROWS, 3 * DATES, dtype=BF16),
-        ),
+        struct(DATES + OUT_ROWS + IFGS, 3 * DATES, dtype=BF16),
         [full()],
-        (full(), full(), full()),
-        flops=30 * 6 * 2 * 256**3,
-        nbytes=10**6,
-    )(pairs.T)
-
-    refs = lax.all_gather(cand, "z_lo", axis=0, tiled=True)
-    refs = jnp.sum(refs, axis=0, keepdims=True)
-    refs = lax.all_gather(refs, "z_hi", axis=0, tiled=True)
-    refs = call(rows_kernel, struct(2 * STACK, LANE), [full()], full())(refs)
-    refs, block, operator = lax.optimization_barrier((refs, block, operator))
-    refs = lax.all_to_all(
-        refs,
-        ("x_hi",) + STACK_AXES,
-        split_axis=0,
-        concat_axis=0,
-        tiled=True,
-    )
+        full(),
+        flops=10**4,
+        nbytes=10**4,
+    )(design_t)
 
     high, sums = call(
         invert_kernel,
         (struct(OUT_ROWS, PIXELS), struct(STACK * SUMS, LANE)),
-        [full(pltpu.SMEM)] + [full()] * 6,
+        [full()] * 5,
         (full(), full()),
         flops=6 * 2 * PIXELS * DATES * 1200,
         nbytes=4 * (IFGS + OUT_ROWS) * PIXELS,
     )(
-        lax.axis_index(STACK_AXES).reshape(1),
         block.reshape(IFGS * SUB, LANE),
         refs,
-        design,
         design_t,
         operator,
-        coherent,
+        mask_tile,
     )
 
     count = SPACE

time: 89.3 us -> 90.2 us (1.010)
  blocking collectives: 55.3 us -> 62.5 us
  waiting for transfers between devices: 5.48 us -> 0.16 us
  starting transfers between devices: 13.7 us -> 12.6 us
    all_gather x2 -> x3, blocking collectives: 29.9 us -> 35.6 us  [the longest x2 29.9 us: body(): lax.all_gather(refs, axis, axis=0, tiled=True)]
    all_to_all x1, waiting for transfers between devices: 5.47 us -> 0.15 us  [body(): lax.all_to_all(refs, STACK_AXES, split_axis=0, concat_axis=0, tiled=True)]
    all_to_all x1, blocking collectives: 25.4 us -> 27 us  [body(): lax.all_to_all(pieces.reshape(STACK, PIECE, SUB, LANE), STACK_AXES, split...]
    all_to_all x1, starting transfers between devices: 7.1 us -> 5.73 us  [body(): lax.all_to_all(refs, STACK_AXES, split_axis=0, concat_axis=0, tiled=True)]
    pallas_call x2 -> x4, Pallas kernels: 5.09 us -> 5.15 us  [the longest x1 4.47 us: body(): call(operator_kernel, struct(DATES + OUT_ROWS + IFGS, 3 * DATES, dtype=BF...]
where the time goes in v4:
time: 90.2 us; the launch traced here: 89.4 us
  blocking collectives  62.5 us (69%)
  Pallas kernels  12.7 us (14%)
  starting transfers between devices  12.6 us (14%)
  between operations  1.39 us (2%)
    all_gather x2, blocking collectives, body(): lax.all_gather(refs, axis, axis=0, tiled=True)  29.9 us
    all_to_all x1, blocking collectives, body(): lax.all_to_all(pieces.reshape(STACK, PIECE, SUB, LANE), STACK_AXES, split...  27 us
    all_to_all x1, starting transfers between devices, body(): lax.all_to_all(send, STACK_AXES, split_axis=0, concat_axis=0, tiled=True)  6.09 us
    all_to_all x1, starting transfers between devices, body(): lax.all_to_all(refs, STACK_AXES, split_axis=0, concat_axis=0, tiled=True)  5.73 us
    all_gather x1, blocking collectives, body(): refs = lax.all_gather(refs, 'x_hi', axis=0, tiled=True)  5.71 us
    pallas_call x1, Pallas kernels, body(): call(operator_kernel, struct(DATES + OUT_ROWS + IFGS, 3 * DATES, dtype=BF...  4.47 us
    pallas_call x1, Pallas kernels, body(): call(pack_kernel, (struct(STACK, OWN_IFGS, SUB, LANE), struct(1, LANE)),...  3.23 us
    pallas_call x1, Pallas kernels, body(): call(invert_kernel, (struct(OUT_ROWS, PIXELS), struct(STACK * SUMS, LANE)...  2.86 us
  transfers between devices with their start and end apart: 3, of which 1 were waited for; matrix products, arithmetic and copies ran while one was open for 0% of the time, Pallas kernels for 6%

profile of v4, /device:TPU:6, one launch (start us, length us, event | category | flops | bytes accessed | tf_op | source)
XLA Modules:
  0.0 89.4 jit_solution(15602377803303220847)
XLA Ops:
  1.3 3.2 %shard_map.59 = (f32[16,36,8,128]{3,2,1,0:T(8,128)}, f32[1,128]{1,0:T(1,128)}) custom-call(s32[1]{0:T(128)S(6)} %copy.8.pixel_ref, s32[1]{0:T(128)} %bitcast.space_ref, f32[36,16,1024]{2,1,0:T(8,128)} %x_ref.1), custom_call_target="tpu_custom_call" | custom-call | bytes 4718592 | tf_op jit(solution)/shard_map/pallas_call | solution.py:278
  4.5 0.0 copy-start.2
  4.5 0.0 copy-start.3
  4.5 0.0 copy-start
  4.6 6.1 %all-to-all-start = ((f32[16,36,8,128]{3,2,1,0:T(8,128)}), f32[16,36,8,128]{3,2,1,0:T(8,128)S(1)}, u32[]{:S(2)}, u32[]{:S(2)}) async-start(f32[16,36,8,128]{3,2,1,0:T(8,128)} %get-tuple-element.11), calls=%async_computation | async-start | bytes 4718592 | tf_op jit(solution)/shard_map/all_to_all | solution.py:291
  10.7 0.0 copy-done.2
  10.7 0.1 shard_map.61.design_t_ref
  10.7 0.0 copy-done.3
  10.7 12.1 %all-gather.2 = f32[4,1,128]{2,1,0:T(1,128)S(1)} all-gather(f32[1,1,128]{2,1,0:T(1,128)S(1)} %bitcast.19), channel_id=1, replica_groups=mesh['y'=4,'x_lo'=2,'core'=2,'x_hi'=2,'z_hi'=4,'z_lo'=4] {'z_lo'}, dimensions={0}, use_global_device_ids=true | all-gather | bytes 2560 | tf_op jit(solution)/shard_map/all_gather | solution.py:304
  22.9 17.7 %all-gather.3 = f32[4,1,128]{2,1,0:T(1,128)S(1)} all-gather(f32[1,1,128]{2,1,0:T(1,128)S(1)} %bitcast.18), channel_id=2, replica_groups=mesh['y'=4,'x_lo'=2,'core'=2,'x_hi'=2,'z_hi'=4,'z_lo'=4] {'z_hi'}, dimensions={0}, use_global_device_ids=true | all-gather | bytes 2560 | tf_op jit(solution)/shard_map/all_gather | solution.py:304
  40.6 5.7 %all-gather.4 = f32[2,1,128]{2,1,0:T(1,128)S(1)} all-gather(f32[1,1,128]{2,1,0:T(1,128)S(1)} %bitcast.20), channel_id=3, replica_groups=mesh['y'=4,'x_lo'=2,'core'=2,'x_hi'=2,'z_hi'=4,'z_lo'=4] {'x_hi'}, dimensions={0}, use_global_device_ids=true | all-gather | bytes 1536 | tf_op jit(solution)/shard_map/all_gather | solution.py:305
  46.4 0.6 shard_map.60
  47.0 0.0 copy-done
  47.0 0.0 all-to-all-done
  47.0 5.7 %all-to-all-start.1 = ((f32[16,1,128]{2,1,0:T(1,128)}), f32[16,1,128]{2,1,0:T(1,128)S(1)}, u32[]{:S(2)}, u32[]{:S(2)}) async-start(f32[16,1,128]{2,1,0:T(1,128)} %bitcast.9), calls=%async_computation.1 | async-start | bytes 16384 | tf_op jit(solution)/shard_map/all_to_all | solution.py:313
  52.7 4.5 %shard_map.63.op_ref = bf16[976,432]{1,0:T(8,128)(2,1)S(1)} custom-call(bf16[144,576]{1,0:T(8,128)(2,1)S(1)} %shard_map.61.design_t_ref), custom_call_target="tpu_custom_call" | custom-call | flops 10000 | bytes 10000 | tf_op jit(solution)/shard_map/pallas_call | solution.py:315
  57.2 0.2 all-to-all-done.1
  57.3 2.9 %shard_map.64 = (f32[256,1024]{1,0:T(8,128)S(1)}, f32[160,128]{1,0:T(8,128)S(1)}) custom-call(f32[4608,128]{1,0:T(8,128)S(1)} %bitcast.14, f32[16,128]{1,0:T(8,128)S(1)} %bitcast.15, bf16[144,576]{1,0:T(8,128)(2,1)S(1)} %shard_map.61.design_t_ref, bf16[976,432]{1,0:T(8,128)(2,1)S(1)} %shard_map.63.op_ref, f32[8,128]{1,0:T(8,128)S(1)} %shard_map.62.mask_ref), custom_call_target="tpu_custom_call" | custom-call | flops 2123366400 | bytes 3407872 | tf_op jit(solution)/shard_map/pallas_call | solution.py:324
  60.2 0.0 copy-start.1
  60.2 0.8 collective-permute-start
  61.0 0.0 collective-permute-done.sums_ref
  61.0 0.2 shard_map.65
  61.3 27.0 %all_to_all.21.x_ref = f32[16,12,8,128]{3,2,1,0:T(8,128)S(1)} all-to-all(f32[16,12,8,128]{3,2,1,0:T(8,128)S(1)} %bitcast.13), channel_id=1, replica_groups=mesh['y'=4,'x_lo'=2,'core'=2,'x_hi'=2,'z_hi'=4,'z_lo'=4] {'y','x_lo','co..., dimensions={0} | all-to-all | bytes 1572864 | tf_op jit(solution)/shard_map/all_to_all | solution.py:359
  88.2 1.2 %shard_map.66 = (f32[9,1024]{1,0:T(8,128)}, f32[9,16,1024]{2,1,0:T(8,128)}) custom-call(f32[16,12,8,128]{3,2,1,0:T(8,128)S(1)} %all_to_all.21.x_ref, s32[16,1024]{1,0:T(8,128)S(1)} %copy-done.1), custom_call_target="tpu_custom_call" | custom-call | flops 75497472 | bytes 1572864 | tf_op jit(solution)/shard_map/pallas_call | solution.py:363
  (4 shorter events, 0.0 us)
Async XLA Ops:
  4.5 6.1 %copy-start.2 = (s32[576,2]{0,1:T(2,128)S(1)}, s32[576,2]{0,1:T(2,128)}, u32[]{:S(2)}) copy-start(s32[576,2]{0,1:T(2,128)} %param.5) | copy-start | bytes 13828
  4.5 6.2 %copy-start.3 = (f32[1,128]{1,0:T(1,128)S(1)}, f32[1,128]{1,0:T(1,128)}, u32[]{:S(2)}) copy-start(f32[1,128]{1,0:T(1,128)} %get-tuple-element.10) | copy-start | bytes 1540
  4.5 42.4 %copy-start = (s32[16,1024]{1,0:T(8,128)S(1)}, s32[16,1024]{1,0:T(8,128)}, u32[]{:S(2)}) copy-start(s32[16,1024]{1,0:T(8,128)} %mask_ref.3) | copy-start | bytes 196612
  4.6 42.4 %all-to-all-start = ((f32[16,36,8,128]{3,2,1,0:T(8,128)}), f32[16,36,8,128]{3,2,1,0:T(8,128)S(1)}, u32[]{:S(2)}, u32[]{:S(2)}) async-start(f32[16,36,8,128]{3,2,1,0:T(8,128)} %get-tuple-element.11), calls=%async_computation | async-start | bytes 4718592 | tf_op jit(solution)/shard_map/all_to_all | solution.py:291
  47.0 10.4 %all-to-all-start.1 = ((f32[16,1,128]{2,1,0:T(1,128)}), f32[16,1,128]{2,1,0:T(1,128)S(1)}, u32[]{:S(2)}, u32[]{:S(2)}) async-start(f32[16,1,128]{2,1,0:T(1,128)} %bitcast.9), calls=%async_computation.1 | async-start | bytes 16384 | tf_op jit(solution)/shard_map/all_to_all | solution.py:313
  60.2 28.0 %copy-start.1 = (s32[16,1024]{1,0:T(8,128)S(1)}, s32[16,1024]{1,0:T(8,128)}, u32[]{:S(2)}) copy-start(s32[16,1024]{1,0:T(8,128)} %mask_ref.3) | copy-start | bytes 196612
  60.2 0.8 collective-permute-start
